TPU v7x, 32 devices: a whole 2x2x4 slice. The times are simulated.
32 devices in a mesh: dp: 4 (over z), expert: 8 (over y, x, core).
Axes of the slice: x: 2, y: 2, z: 4, core: 2. Of those that a mesh axis runs over, the one named last changes fastest.
Arguments:
- attn_input: bfloat16 [4096, 3072], P(('dp', 'expert')), may hold values from -6 to 6
- key_cot: bfloat16 [4096, 512], P(('dp', 'expert')), may hold values from -6 to 6
- routing: int32 [4096, 4], P(('dp', 'expert')), may hold values from 0 to 7, all different within a row; in each aligned block of 128 rows (0 to 127, 128 to 255, ...) at most 66 rows name the same one
- router_base: float32 [4096, 8], P(('dp', 'expert')), may hold values from -1.5 to 1.5
- router_weight: bfloat16 [3072, 8], replicated, may hold values from -2 to 2
- expert_rows: bfloat16 [256, 66, 3072], P(('dp', 'expert')), may hold values from -6 to 6
- expert_dots: bfloat16 [256, 66], P(('dp', 'expert')), may hold values from -16 to 16
- key_weight: float32 [3072, 512], P(('dp', 'expert')), may hold values from -0.25 to 0.25
- first_moment: float32 [3072, 512], P(('dp', 'expert')), may hold values from -384 to 384
- second_moment: float32 [3072, 512], P(('dp', 'expert')), may hold values from 819.2 to 20480
Outputs:
- input_grad: bfloat16 [4096, 3072], P(('dp', 'expert'))
- new_key_weight: float32 [3072, 512], P(('dp', 'expert'))
- new_first_moment: float32 [3072, 512], P(('dp', 'expert'))
- new_second_moment: float32 [3072, 512], P(('dp', 'expert'))
Inputs may be any that keep to these rules, and one draw needn't show every extreme that they name: `routing`: each token names 4 different experts. The 128 tokens of one device name any one expert at most 66 times, and that bound is reached.
All inputs are finite; a program needn't handle non-finite values.
Results may differ from a plain program's by a relative error of at most 0.0043.
Values may be sent and summed in bfloat16 or wider, within the bound.
A program may use at most 64 MiB of HBM per device.

v0:
```python
import jax
import jax.numpy as jnp
from jax import lax
from jax.sharding import PartitionSpec as P

ADAM_STEP = 10


beta_one = 0.9
beta_two = 0.95
epsilon = 1e-08
learn_rate = 0.005
decay_rate = 0.1
routed_offset = 3.5


def route_slots(routing, experts, capacity):
    choose = (routing[:, :, None] == jnp.arange(experts, dtype=jnp.int32)[None, None, :]).astype(
        jnp.int32
    )
    per_expert = jnp.sum(choose, axis=1)
    before = jnp.cumsum(per_expert, axis=0) - per_expert
    slots = jnp.sum(choose * before[:, None, :], axis=2)
    return (choose, routing * capacity + slots)


def combine(routing, router_base, returned, returned_dots, router_weight):
    experts, capacity, features = returned.shape
    choose, flat_index = route_slots(routing, experts, capacity)
    routed_mask = jnp.sum(choose, axis=1).astype(jnp.float32)
    router_probs = jax.nn.softmax(router_base + routed_offset * routed_mask, axis=-1)
    picked = jnp.take(returned.reshape(experts * capacity, features), flat_index, axis=0)
    inner = jnp.take(returned_dots.reshape(experts * capacity), flat_index, axis=0).astype(
        jnp.float32
    )
    chosen = jnp.take_along_axis(router_probs, routing, axis=1)
    chosen_sum = jnp.sum(chosen, axis=1, keepdims=True)
    gate_share = chosen / chosen_sum
    mixed = gate_share[:, 0:1] * picked[:, 0].astype(jnp.float32)
    for position in range(1, routing.shape[1]):
        mixed = mixed + gate_share[:, position : position + 1] * picked[:, position].astype(
            jnp.float32
        )
    mean_inner = jnp.sum(gate_share * inner, axis=1, keepdims=True)
    d_chosen = (inner - mean_inner) / chosen_sum
    d_probs = jnp.sum(choose.astype(jnp.float32) * d_chosen[:, :, None], axis=1)
    d_logits = router_probs * (d_probs - jnp.sum(router_probs * d_probs, axis=1, keepdims=True))
    router_term = jnp.dot(
        d_logits, router_weight.astype(jnp.float32).T, precision=lax.Precision.HIGHEST
    )
    return mixed + router_term


def adamw(weight, first, second, grad):
    new_first = beta_one * first + (1.0 - beta_one) * grad
    new_second = beta_two * second + (1.0 - beta_two) * grad * grad
    first_hat = new_first / (1.0 - beta_one**ADAM_STEP)
    second_hat = new_second / (1.0 - beta_two**ADAM_STEP)
    new_weight = weight - learn_rate * (
        first_hat / (jnp.sqrt(second_hat) + epsilon) + decay_rate * weight
    )
    return (new_weight, new_first, new_second)


def local(
    attn_input,
    key_cot,
    routing,
    router_base,
    router_weight,
    expert_rows,
    expert_dots,
    key_weight,
    first_moment,
    second_moment,
):
    returned, returned_dots = (
        lax.all_to_all(expert_rows, "expert", split_axis=0, concat_axis=0, tiled=True),
        lax.all_to_all(expert_dots, "expert", split_axis=0, concat_axis=0, tiled=True),
    )
    moe_term = combine(routing, router_base, returned, returned_dots, router_weight)
    key_term = lax.dot_general(
        key_cot,
        lax.all_gather(key_weight.astype(jnp.bfloat16), ("dp", "expert"), axis=0, tiled=True),
        (((1,), (1,)), ((), ())),
        preferred_element_type=jnp.float32,
    )
    input_grad = (moe_term + key_term).astype(jnp.bfloat16)
    partial_grad = lax.dot_general(
        attn_input, key_cot, (((0,), (0,)), ((), ())), preferred_element_type=jnp.float32
    )
    cycle_size = lax.axis_size("dp")
    group_size = lax.axis_size("expert")
    shard_rows = key_weight.shape[0]
    stacked = partial_grad.reshape(cycle_size, group_size * shard_rows, partial_grad.shape[1])
    halfway = lax.psum_scatter(stacked.astype(jnp.bfloat16), "dp", scatter_dimension=0, tiled=True)
    summed = lax.psum_scatter(halfway, "expert", scatter_dimension=1, tiled=True).astype(
        jnp.float32
    )
    key_grad = summed.reshape(shard_rows, partial_grad.shape[1])
    new_key_weight, new_first_moment, new_second_moment = adamw(
        key_weight, first_moment, second_moment, key_grad
    )
    return (input_grad, new_key_weight, new_first_moment, new_second_moment)


def solution(mesh):
    in_specs = (
        P(("dp", "expert"), None),
        P(("dp", "expert"), None),
        P(("dp", "expert"), None),
        P(("dp", "expert"), None),
        P(),
        P(("dp", "expert"), None, None),
        P(("dp", "expert"), None),
        P(("dp", "expert"), None),
        P(("dp", "expert"), None),
        P(("dp", "expert"), None),
    )
    out_specs = (
        P(("dp", "expert"), None),
        P(("dp", "expert"), None),
        P(("dp", "expert"), None),
        P(("dp", "expert"), None),
    )
    return jax.shard_map(local, mesh=mesh, in_specs=in_specs, out_specs=out_specs, check_vma=False)
```

profile of v0, /device:TPU:0, one launch (start us, length us, event | category | flops | bytes accessed | tf_op | source)
XLA Modules:
  0.0 217.3 jit_solution(14931417842711804464)
XLA Ops:
  7.2 0.0 copy-start
  7.2 0.0 copy-start.2
  7.2 0.0 copy-start.3
  7.2 0.0 copy-start.4
  7.2 0.0 reduce-scatter.3.cloned.1.call-start
  7.3 1.0 copy-done
  8.3 3.6 %convolution_convert_fusion = bf16[3072,512]{1,0:T(8,128)(2,1)} fusion(bf16[128,3072]{1,0:T(8,128)(2,1)S(1)} %copy-done, bf16[128,512]{1,0:T(8,128)(2,1)} %param.11), kind=kOutput, calls=%fused_computation.3 | convolution fusion | flops 404226048 | bytes 4063232 | tf_op jit(solution)/shard_map/dot_general | solution.py:89
  11.9 0.0 reduce-scatter.3.cloned.1.call-update
  11.9 0.0 reduce-scatter.5.cloned.1.call-start
  12.0 63.1 %reduce-scatter.3.cloned.1.call-done = bf16[1,768,512]{2,1,0:T(8,128)(2,1)} async-done(((bf16[4,768,512]{2,1,0:T(8,128)(2,1)}), bf16[1,768,512]{2,1,0:T(8,128)(2,1)}) %reduce-scatter.3.cloned.1.call-update) | async-done | bytes 786448 | tf_op jit(solution)/shard_map/reduce_scatter | solution.py:96
  75.0 0.0 reduce-scatter.5.cloned.1.call-update
  75.1 0.0 all-gather.2.cloned.1.call-start
  75.1 38.1 %reduce-scatter.5.cloned.1.call-done = bf16[1,96,512]{2,1,0:T(8,128)(2,1)} async-done(((bf16[1,768,512]{2,1,0:T(8,128)(2,1)}), bf16[1,96,512]{2,1,0:T(8,128)(2,1)}) %reduce-scatter.5.cloned.1.call-update) | async-done | bytes 98320 | tf_op jit(solution)/shard_map/reduce_scatter | solution.py:97
  113.2 0.0 copy-done.2
  113.2 0.0 copy-done.3
  113.2 0.0 copy-done.4
  113.2 1.8 multiply_subtract_fusion
  115.0 0.0 all-gather.2.cloned.1.call-update
  115.0 0.0 copy-done.7
  115.0 0.6 copy.122
  115.6 3.3 %all-to-all-start.1 = ((bf16[8,1,66]{2,1,0:T(2,128)(2,1)}), bf16[8,1,66]{2,1,0:T(2,128)(2,1)S(1)}, u32[]{:S(2)}, u32[]{:S(2)}) async-start(bf16[8,1,66]{2,1,0:T(2,128)(2,1)} %copy.122), calls=%async_computation.1 | async-start | bytes 8192 | tf_op jit(solution)/shard_map/all_to_all | solution.py:79
  119.0 5.5 %copy.119 = bf16[8,66,3072]{2,1,0:T(8,128)(2,1)} copy(bf16[8,66,3072]{2,0,1:T(8,128)(2,1)} %param.15) | data formatting | bytes 6488064 | tf_op args[5]
  124.5 0.0 all-to-all-done.1
  124.5 4.8 %all-to-all-start = ((bf16[8,66,3072]{2,1,0:T(8,128)(2,1)}), bf16[8,66,3072]{2,1,0:T(8,128)(2,1)}, u32[]{:S(2)}, u32[]{:S(2)}) async-start(bf16[8,66,3072]{2,1,0:T(8,128)(2,1)} %copy.119), calls=%async_computation | async-start | bytes 7077888 | tf_op jit(solution)/shard_map/all_to_all | solution.py:78
  129.3 0.0 copy-done.5
  129.4 0.1 copy.114
  129.5 0.1 reshape.106
  129.6 0.1 copy.116
  129.7 0.0 copy-done.6
  129.8 2.5 %gather_fusion.2 = f32[512]{0:T(512)S(1)} fusion(f32[128,8]{0,1:T(8,128)S(1)} %fusion.11, s32[512]{0:T(512)S(1)} %reshape.106), kind=kCustom, calls=%fused_computation.2 | custom fusion | bytes 8192 | tf_op jit(solution)/shard_map/jit(take_along_axis)/gather | solution.py:36
  132.3 0.1 reshape.109
  132.4 0.1 copy.115
  132.5 0.2 reduce_window_sum.11
  132.8 0.1 copy.120
  132.9 0.1 reshape.92
  133.1 0.1 reshape.81
  133.2 3.5 %gather_fusion.1 = bf16[512]{0:T(512)(128)(2,1)S(1)} fusion(bf16[528]{0:T(1024)(128)(2,1)S(1)} %reshape.81, s32[1024]{0:T(1024)S(1)} %pad_clamp_fusion), kind=kCustom, calls=%fused_computation.1 | custom fusion | bytes 4096 | tf_op jit(solution)/shard_map/jit(_take)/gather | solution.py:33
  136.7 0.1 reshape.99
  136.8 0.1 copy.123
  137.0 41.8 %all-to-all-done = bf16[8,66,3072]{2,1,0:T(8,128)(2,1)} async-done(((bf16[8,66,3072]{2,1,0:T(8,128)(2,1)}), bf16[8,66,3072]{2,1,0:T(8,128)(2,1)}, u32[]{:S(2)}, u32[]{:S(2)}) %all-to-all-start) | async-done | bytes 3244064 | tf_op jit(solution)/shard_map/all_to_all | solution.py:78
  178.8 3.7 %reshape.80 = bf16[528,3072]{1,0:T(8,128)(2,1)} reshape(bf16[8,66,3072]{2,1,0:T(8,128)(2,1)} %all-to-all-done) | data formatting | bytes 6488064 | tf_op jit(solution)/shard_map/reshape | solution.py:32
  182.4 9.4 %gather_fusion = bf16[512,3072]{1,0:T(8,128)(2,1)} fusion(bf16[528,3072]{1,0:T(8,128)(2,1)} %reshape.80, s32[1024]{0:T(1024)S(1)} %pad_clamp_fusion), kind=kCustom, calls=%fused_computation | custom fusion | bytes 6293504 | tf_op jit(solution)/shard_map/jit(_take)/gather | solution.py:32
  191.8 6.1 %reshape.91 = bf16[128,4,3072]{2,1,0:T(4,128)(2,1)} reshape(bf16[512,3072]{1,0:T(8,128)(2,1)} %gather_fusion) | data formatting | bytes 6291456 | tf_op jit(solution)/shard_map/jit(_take)/gather | solution.py:32
  197.9 5.6 %copy_select_fusion = bf16[128,4,3072]{2,0,1:T(8,128)(2,1)} fusion(bf16[128,4,3072]{2,1,0:T(4,128)(2,1)} %reshape.91, pred[128,4]{0,1:T(4,128)(4,1)S(1)} %get-tuple-element.9), kind=kLoop, calls=%fused_computation.7 | loop fusion | flops 1572864 | bytes 6291968 | tf_op jit(solution)/shard_map/jit(_take)/select_n | solution.py:32
  203.6 0.0 copy-done.1
  203.6 3.0 %fusion.20 = f32[128,3072]{1,0:T(8,128)S(1)} fusion(bf16[128,512]{1,0:T(8,128)(2,1)S(1)} %copy-done.1, bf16[3072,512]{1,0:T(8,128)(2,1)} %all-gather.2.cloned.1.call-done), kind=kOutput, calls=%fused_computation.56 | convolution fusion | flops 402653184 | bytes 4849664 | tf_op jit(solution)/shard_map/dot_general | solution.py:82
  206.6 0.0 copy-done.8
  206.6 4.2 %fusion.1 = bf16[128,3072]{1,0:T(8,128)(2,1)} fusion(f32[128,3072]{1,0:T(8,128)S(1)} %fusion.20, bf16[3072,8]{0,1:T(8,128)(2,1)S(1)} %copy-done.8, bf16[128,4,3072]{2,0,1:T(8,128)(2,1)} %copy_select_fusion, f32[128]{0:T(128)S(1)} %get-tuple-element.12, f32[128]{0:T(128)S(1)} %get-tuple-element.13, f32[128]{0:T(128)S(1)} %get-tuple-element.14, ...), kind=kOutput, calls=%fused_computation.6 | convolution fusion | flops 43255808 | bytes 5564928 | tf_op jit(solution)/shard_map/dot_general | solution.py:48
  (23 shorter events, 0.3 us)
Async XLA Ops:
  7.2 1.1 copy-start
  7.2 106.0 %copy-start.2 = (f32[96,512]{1,0:T(8,128)S(1)}, f32[96,512]{1,0:T(8,128)}, u32[]{:S(2)}) copy-start(f32[96,512]{1,0:T(8,128)} %param.17) | copy-start | bytes 589828
  7.2 106.0 %copy-start.3 = (f32[96,512]{1,0:T(8,128)S(1)}, f32[96,512]{1,0:T(8,128)}, u32[]{:S(2)}) copy-start(f32[96,512]{1,0:T(8,128)} %param.18) | copy-start | bytes 589828
  7.2 106.0 %copy-start.4 = (f32[96,512]{1,0:T(8,128)S(1)}, f32[96,512]{1,0:T(8,128)}, u32[]{:S(2)}) copy-start(f32[96,512]{1,0:T(8,128)} %param.19) | copy-start | bytes 589828
  7.2 67.8 %reduce-scatter.3.cloned.1.call-start = ((), (), s32[]{:S(2)}) async-start(), calls=%async_computation.5 | async-start | bytes 3932160 | tf_op jit(solution)/shard_map/reduce_scatter | solution.py:96
  11.9 103.2 %copy-start.7 = (bf16[8,66]{1,0:T(8,128)(2,1)S(1)}, bf16[8,66]{1,0:T(8,128)(2,1)}, u32[]{:S(2)}) copy-start(bf16[8,66]{1,0:T(8,128)(2,1)} %param.16) | copy-start | bytes 3172
  11.9 101.3 %reduce-scatter.5.cloned.1.call-start = ((), (), s32[]{:S(2)}) async-start(), calls=%async_computation.6 | async-start | bytes 884736 | tf_op jit(solution)/shard_map/reduce_scatter | solution.py:97
  75.1 128.5 %all-gather.2.cloned.1.call-start = ((), (), s32[]{:S(2)}) async-start(), calls=%async_computation.4 | async-start | bytes 3244032 | tf_op jit(solution)/shard_map/all_gather | solution.py:84
  115.6 8.9 %all-to-all-start.1 = ((bf16[8,1,66]{2,1,0:T(2,128)(2,1)}), bf16[8,1,66]{2,1,0:T(2,128)(2,1)S(1)}, u32[]{:S(2)}, u32[]{:S(2)}) async-start(bf16[8,1,66]{2,1,0:T(2,128)(2,1)} %copy.122), calls=%async_computation.1 | async-start | bytes 8192 | tf_op jit(solution)/shard_map/all_to_all | solution.py:79
  124.5 4.8 %copy-start.5 = (s32[128,4]{0,1:T(4,128)S(1)}, s32[128,4]{0,1:T(4,128)}, u32[]{:S(2)}) copy-start(s32[128,4]{0,1:T(4,128)} %param.12) | copy-start | bytes 6148
  124.5 5.2 %copy-start.6 = (f32[128,8]{0,1:T(8,128)S(1)}, f32[128,8]{0,1:T(8,128)}, u32[]{:S(2)}) copy-start(f32[128,8]{0,1:T(8,128)} %param.13) | copy-start | bytes 12292
  124.5 54.2 %all-to-all-start = ((bf16[8,66,3072]{2,1,0:T(8,128)(2,1)}), bf16[8,66,3072]{2,1,0:T(8,128)(2,1)}, u32[]{:S(2)}, u32[]{:S(2)}) async-start(bf16[8,66,3072]{2,1,0:T(8,128)(2,1)} %copy.119), calls=%async_computation | async-start | bytes 7077888 | tf_op jit(solution)/shard_map/all_to_all | solution.py:78
  197.9 5.6 %copy-start.1 = (bf16[128,512]{1,0:T(8,128)(2,1)S(1)}, bf16[128,512]{1,0:T(8,128)(2,1)}, u32[]{:S(2)}) copy-start(bf16[128,512]{1,0:T(8,128)(2,1)} %param.11) | copy-start | bytes 393220
  203.6 3.1 %copy-start.8 = (bf16[3072,8]{0,1:T(8,128)(2,1)S(1)}, bf16[3072,8]{0,1:T(8,128)(2,1)}, u32[]{:S(2)}) copy-start(bf16[3072,8]{0,1:T(8,128)(2,1)} %param.14) | copy-start | bytes 147460
Sparse Core Ops, SparseCore 0:
  12.0 62.9 reduce-scatter.2
  78.2 34.9 reduce-scatter.4
  116.6 71.7 all-gather.1
where the time goes:
time: 218 us; the launch traced here: 217 us
  waiting for transfers between devices  143 us (66%)
  local copies, waits for them, and re-layouts  33.5 us (15%)
  between operations  13.9 us (6%)
  matrix products  10.8 us (5%)
  starting transfers between devices  8.26 us (4%)
  other arithmetic  7.9 us (4%)
    reduce_scatter x1, waiting for transfers between devices, local(): lax.psum_scatter(stacked.astype(jnp.bfloat16), 'dp', scatter_dimension=0,...  63.1 us
    all_to_all x1, waiting for transfers between devices, local(): lax.all_to_all(expert_rows, 'expert', split_axis=0, concat_axis=0, tiled=...  41.8 us
    reduce_scatter x1, waiting for transfers between devices, local(): lax.psum_scatter(halfway, 'expert', scatter_dimension=1, tiled=True)  38.1 us
    gather x2, local copies, waits for them, and re-layouts, combine(): jnp.take(returned.reshape(experts * capacity, features), flat_index, axis=0)  15.5 us
    unnamed x19, local copies, waits for them, and re-layouts  6.62 us
    select_n x2, other arithmetic, combine(): jnp.take(returned.reshape(experts * capacity, features), flat_index, axis=0)  5.63 us
    all_to_all x1, starting transfers between devices, local(): lax.all_to_all(expert_rows, 'expert', split_axis=0, concat_axis=0, tiled=...  4.81 us
  transfers between devices with their start and end apart: 5, of which 3 were waited for; matrix products, arithmetic and copies ran while one was open for 18% of the time, Pallas kernels for 0%

commit v1 on v0

--- a/solution.py
+++ b/solution.py
@@ -1,6 +1,10 @@
+import functools
+
 import jax
 import jax.numpy as jnp
 from jax import lax
+from jax.experimental import pallas as pl
+from jax.experimental.pallas import tpu as pltpu
 from jax.sharding import PartitionSpec as P
 
 ADAM_STEP = 10
@@ -104,7 +108,399 @@
     return (input_grad, new_key_weight, new_first_moment, new_second_moment)
 
 
+MESH = pl.DeviceIdType.MESH
+CONTRACT_FIRST = (((0,), (0,)), ((), ()))
+CONTRACT_LAST = (((1,), (1,)), ((), ()))
+
+
+def split_rows(values):
+    high = values.astype(jnp.bfloat16)
+    low = (values - high.astype(jnp.float32)).astype(jnp.bfloat16)
+    return jnp.concatenate([high, low], axis=0)
+
+
+def fused(
+    attn_hbm,
+    cot_ref,
+    routing_ref,
+    base_ref,
+    router_ref,
+    rows_hbm,
+    dots_ref,
+    weight_ref,
+    first_ref,
+    second_ref,
+    out_ref,
+    new_weight_ref,
+    new_first_ref,
+    new_second_ref,
+    attn_pair,
+    cot_pair,
+    rows_got,
+    dots_send,
+    dots_got,
+    wide,
+    grad_send,
+    grad_got,
+    grad_own,
+    cross_send,
+    cross_got,
+    total,
+    half_got,
+    share,
+    acc,
+    rows_ss,
+    rows_rs,
+    dots_ss,
+    dots_rs,
+    pair_ss,
+    pair_rs,
+    wz_ss,
+    wz_rs,
+    wx_ss,
+    wx_rs,
+    wc_ss,
+    wc_rs,
+    gz_ss,
+    gz_rs,
+    gx_ss,
+    gx_rs,
+    gc_ss,
+    gc_rs,
+    local_sem,
+):
+    tokens, features = acc.shape
+    experts, capacity, _ = rows_got.shape
+    layers, slab, keys = wide.shape
+    shard = weight_ref.shape[0]
+    half = keys // 2
+    z, e = lax.axis_index("dp"), lax.axis_index("expert")
+    y, x, c = e // 4, (e // 2) % 2, e % 2
+
+    def peer(r):
+        return ((y + r // 4) % 2) * 4 + ((x + (r // 2) % 2) % 2) * 2 + (c + r % 2) % 2
+
+    def rows_of(owner):
+        return pl.ds(pl.multiple_of(owner * shard, 32), shard)
+
+    def columns(start, size):
+        return pl.ds(pl.multiple_of(start, 256), size)
+
+    def remote(src, dst, send_sem, recv_sem, to):
+        copy = pltpu.make_async_remote_copy(
+            src_ref=src,
+            dst_ref=dst,
+            send_sem=send_sem,
+            recv_sem=recv_sem,
+            device_id=to,
+            device_id_type=MESH,
+        )
+        copy.start()
+        return copy
+
+    barrier = pltpu.get_barrier_semaphore()
+    for r in range(1, experts):
+        pl.semaphore_signal(barrier, inc=1, device_id=(z, peer(r)), device_id_type=MESH)
+    for rz in range(1, layers):
+        pl.semaphore_signal(
+            barrier, inc=1, device_id=((z + rz) % layers, e), device_id_type=MESH
+        )
+    own_attn = pltpu.make_async_copy(attn_hbm, attn_pair.at[pl.ds(0, tokens)], local_sem.at[0])
+    own_attn.start()
+    own_rows = pltpu.make_async_copy(rows_hbm.at[e], rows_got.at[0], local_sem.at[1])
+    own_rows.start()
+    wide[z, rows_of(e), :] = weight_ref[...].astype(jnp.bfloat16)
+    dots_all = dots_ref[...].astype(jnp.float32)
+    dots_send[...] = jnp.zeros_like(dots_send)
+    for j in range(experts):
+        dots_send[j, :, 0:capacity] = jnp.broadcast_to(dots_all[j : j + 1, :], (8, capacity))
+    cot_pair[0:tokens, :] = cot_ref[:, columns(c * half, half)]
+    pl.semaphore_wait(barrier, experts - 1 + layers - 1)
+
+    twin = (z, peer(1))
+    pair = [
+        remote(
+            attn_hbm, attn_pair.at[pl.ds(tokens, tokens)], pair_ss.at[0], pair_rs.at[0], twin
+        ),
+        remote(
+            cot_ref.at[:, columns((1 - c) * half, half)],
+            cot_pair.at[pl.ds(tokens, tokens)],
+            pair_ss.at[1],
+            pair_rs.at[1],
+            twin,
+        ),
+    ]
+    mine = wide.at[z, rows_of(e)]
+    along = [
+        remote(mine, mine, wz_ss.at[rz], wz_rs.at[rz], ((z + rz) % layers, e))
+        for rz in range(1, layers)
+    ]
+    dots = {}
+    for r in range(1, experts):
+        dots[r] = remote(
+            dots_send.at[peer(r)], dots_got.at[r], dots_ss.at[r], dots_rs.at[r], (z, peer(r))
+        )
+    rows = {}
+    for r in range(1, experts):
+        rows[r] = remote(
+            rows_hbm.at[peer(r)], rows_got.at[r], rows_ss.at[r], rows_rs.at[r], (z, peer(r))
+        )
+
+    own_attn.wait()
+    for copy in pair:
+        copy.wait_recv()
+
+    def partial(layer):
+        return lax.dot_general(
+            attn_pair[:, columns(layer * slab, slab)],
+            cot_pair[...],
+            CONTRACT_FIRST,
+            preferred_element_type=jnp.float32,
+        )
+
+    outward = {}
+    for rz in (2, 1, 3):
+        to = (z + rz) % layers
+        grad_send[rz] = partial(to).astype(jnp.bfloat16)
+        outward[rz] = remote(
+            grad_send.at[rz], grad_got.at[rz], gz_ss.at[rz], gz_rs.at[rz], (to, e)
+        )
+    grad_own[...] = partial(z)
+
+    lanes = lax.broadcasted_iota(jnp.int32, (tokens, experts), 1)
+    routing = routing_ref[...]
+    choose = jnp.zeros((tokens, experts), jnp.float32)
+    for k in range(routing.shape[1]):
+        choose = choose + (routing[:, k : k + 1] == lanes).astype(jnp.float32)
+    earlier = (
+        lax.broadcasted_iota(jnp.int32, (tokens, tokens), 1)
+        < lax.broadcasted_iota(jnp.int32, (tokens, tokens), 0)
+    ).astype(jnp.bfloat16)
+    before = jnp.dot(
+        earlier, choose.astype(jnp.bfloat16), preferred_element_type=jnp.float32
+    ).astype(jnp.int32)
+    place = jnp.where(choose > 0.0, before, -1)
+    logits = base_ref[...] + routed_offset * choose
+    raised = jnp.exp(logits - jnp.max(logits, axis=1, keepdims=True))
+    probs = raised / jnp.sum(raised, axis=1, keepdims=True)
+    chosen = probs * choose
+    chosen_sum = jnp.sum(chosen, axis=1, keepdims=True)
+    gate = chosen / chosen_sum
+
+    for copy in along:
+        copy.wait_recv()
+    column = wide.at[:, rows_of(e)]
+    across = {
+        q: remote(column, column, wx_ss.at[q], wx_rs.at[q], (z, peer(2 * q)))
+        for q in range(1, 4)
+    }
+    swap = {0: remote(column, column, wc_ss.at[0], wc_rs.at[0], twin)}
+
+    inner = jnp.zeros((tokens, experts), jnp.float32)
+    slots = lax.broadcasted_iota(jnp.int32, (tokens, capacity), 1)
+    for r in range(experts):
+        if r > 0:
+            dots[r].wait_recv()
+            got = dots_got[r, 0:1, 0:capacity]
+        else:
+            got = dots_send[e, 0:1, 0:capacity]
+        this = lanes == peer(r)
+        place_r = jnp.sum(jnp.where(this, place, 0), axis=1, keepdims=True)
+        gate_r = jnp.sum(jnp.where(this, gate, 0.0), axis=1, keepdims=True)
+        hit = slots == place_r
+        share[r] = split_rows(jnp.where(hit, gate_r, 0.0))
+        inner_r = jnp.sum(jnp.where(hit, got, 0.0), axis=1, keepdims=True)
+        inner = inner + jnp.where(this, inner_r, 0.0)
+    mean_inner = jnp.sum(gate * inner, axis=1, keepdims=True)
+    d_probs = choose * (inner - mean_inner) / chosen_sum
+    d_logits = probs * (d_probs - jnp.sum(probs * d_probs, axis=1, keepdims=True))
+    d_parts = split_rows(d_logits)
+
+    def router_tile(i, _):
+        here = columns(i * slab, slab)
+        both = lax.dot_general(
+            d_parts, router_ref[here, :], CONTRACT_LAST, preferred_element_type=jnp.float32
+        )
+        acc[:, here] = both[:tokens] + both[tokens:]
+        return 0
+
+    lax.fori_loop(0, layers, router_tile, 0)
+
+    def add_rows(r):
+        def tile(i, _):
+            here = columns(i * slab, slab)
+            both = jnp.dot(
+                share[r], rows_got[r, :, here], preferred_element_type=jnp.float32
+            )
+            acc[:, here] += both[:tokens] + both[tokens:]
+            return 0
+
+        lax.fori_loop(0, layers, tile, 0)
+
+    own_rows.wait()
+    add_rows(0)
+    rows[1].wait_recv()
+    add_rows(1)
+
+    for q in range(1, 4):
+        across[q].wait_recv()
+        block = wide.at[:, rows_of(peer(2 * q))]
+        swap[q] = remote(block, block, wc_ss.at[q], wc_rs.at[q], twin)
+
+    for rz in range(1, layers):
+        outward[rz].wait_recv()
+    grad_own[...] = (
+        grad_own[...]
+        + grad_got[1].astype(jnp.float32)
+        + grad_got[2].astype(jnp.float32)
+        + grad_got[3].astype(jnp.float32)
+    )
+    inward = {}
+    for q in range(1, 4):
+        chip = pl.ds(pl.multiple_of((peer(2 * q) // 2) * (2 * shard), 32), 2 * shard)
+        cross_send[q] = grad_own[chip, :].astype(jnp.bfloat16)
+        inward[q] = remote(
+            cross_send.at[q], cross_got.at[q], gx_ss.at[q], gx_rs.at[q], (z, peer(2 * q))
+        )
+
+    for q in range(4):
+        swap[q].wait_recv()
+
+    def key_tile(i, _):
+        here = columns(i * slab, slab)
+        acc[:, here] += lax.dot_general(
+            cot_ref[...], wide[i], CONTRACT_LAST, preferred_element_type=jnp.float32
+        )
+        return 0
+
+    lax.fori_loop(0, layers, key_tile, 0)
+
+    for r in (2, 3, 4, 5):
+        rows[r].wait_recv()
+        add_rows(r)
+
+    for q in range(1, 4):
+        inward[q].wait_recv()
+    chip = pl.ds(pl.multiple_of((e // 2) * (2 * shard), 32), 2 * shard)
+    total[...] = (
+        grad_own[chip, :]
+        + cross_got[1].astype(jnp.float32)
+        + cross_got[2].astype(jnp.float32)
+        + cross_got[3].astype(jnp.float32)
+    )
+    last = remote(total.at[rows_of(1 - c)], half_got, gc_ss, gc_rs, twin)
+
+    def update(here, grad):
+        weight, first, second = adamw(
+            weight_ref[:, here], first_ref[:, here], second_ref[:, here], grad
+        )
+        new_weight_ref[:, here] = weight
+        new_first_ref[:, here] = first
+        new_second_ref[:, here] = second
+
+    update(columns(c * half, half), total[rows_of(c), :])
+
+    for r in (6, 7):
+        rows[r].wait_recv()
+        add_rows(r)
+    out_ref[...] = acc[...].astype(jnp.bfloat16)
+    last.wait_recv()
+    update(columns((1 - c) * half, half), half_got[...])
+
+    for copy in [*pair, *along, *dots.values(), *rows.values(), *outward.values()]:
+        copy.wait_send()
+    for copy in [*across.values(), *swap.values(), *inward.values(), last]:
+        copy.wait_send()
+
+
+def fused_local(
+    attn_input,
+    key_cot,
+    routing,
+    router_base,
+    router_weight,
+    expert_rows,
+    expert_dots,
+    key_weight,
+    first_moment,
+    second_moment,
+):
+    tokens, features = attn_input.shape
+    experts, capacity, _ = expert_rows.shape
+    shard, keys = key_weight.shape
+    layers = lax.axis_size("dp")
+    slab, half = features // layers, keys // 2
+    b16, f32 = jnp.bfloat16, jnp.float32
+    vmem, anywhere = pl.BlockSpec(memory_space=pltpu.VMEM), pl.BlockSpec(memory_space=pl.ANY)
+    dma = pltpu.SemaphoreType.DMA
+    return pl.pallas_call(
+        fused,
+        out_shape=(
+            jax.ShapeDtypeStruct((tokens, features), b16),
+            jax.ShapeDtypeStruct((shard, keys), f32),
+            jax.ShapeDtypeStruct((shard, keys), f32),
+            jax.ShapeDtypeStruct((shard, keys), f32),
+        ),
+        in_specs=[anywhere, vmem, vmem, vmem, vmem, anywhere, vmem, vmem, vmem, vmem],
+        out_specs=[vmem] * 4,
+        scratch_shapes=[
+            pltpu.VMEM((2 * tokens, features), b16),
+            pltpu.VMEM((2 * tokens, half), b16),
+            pltpu.VMEM((experts, capacity, features), b16),
+            pltpu.VMEM((experts, 8, 128), f32),
+            pltpu.VMEM((experts, 8, 128), f32),
+            pltpu.VMEM((layers, slab, keys), b16),
+            pltpu.VMEM((layers, slab, half), b16),
+            pltpu.VMEM((layers, slab, half), b16),
+            pltpu.VMEM((slab, half), f32),
+            pltpu.VMEM((4, 2 * shard, half), b16),
+            pltpu.VMEM((4, 2 * shard, half), b16),
+            pltpu.VMEM((2 * shard, half), f32),
+            pltpu.VMEM((shard, half), f32),
+            pltpu.VMEM((experts, 2 * tokens, capacity), b16),
+            pltpu.VMEM((tokens, features), f32),
+            dma((experts,)),
+            dma((experts,)),
+            dma((experts,)),
+            dma((experts,)),
+            dma((2,)),
+            dma((2,)),
+            dma((layers,)),
+            dma((layers,)),
+            dma((4,)),
+            dma((4,)),
+            dma((4,)),
+            dma((4,)),
+            dma((layers,)),
+            dma((layers,)),
+            dma((4,)),
+            dma((4,)),
+            dma,
+            dma,
+            dma((2,)),
+        ],
+        compiler_params=pltpu.CompilerParams(
+            collective_id=0, has_side_effects=True, vmem_limit_bytes=40 * 1024 * 1024
+        ),
+        cost_estimate=pl.CostEstimate(
+            flops=4 * 10**9, bytes_accessed=10**7, transcendentals=10**5
+        ),
+    )(
+        attn_input,
+        key_cot,
+        routing,
+        router_base,
+        router_weight,
+        expert_rows,
+        expert_dots,
+        key_weight,
+        first_moment,
+        second_moment,
+    )
+
+
 def solution(mesh):
+    fits = mesh.shape["dp"] == 4 and mesh.shape["expert"] == 8
     in_specs = (
         P(("dp", "expert"), None),
         P(("dp", "expert"), None),
@@ -123,4 +519,5 @@
         P(("dp", "expert"), None),
         P(("dp", "expert"), None),
     )
-    return jax.shard_map(local, mesh=mesh, in_specs=in_specs, out_specs=out_specs, check_vma=False)
+    return jax.shard_map(
+        fused_local if fits else local, mesh=mesh, in_specs=in_specs, out_specs=out_specs, check_vma=False)

time: 218 us -> 83.4 us (0.38)
  waiting for transfers between devices: 143 us -> 0 us
  Pallas kernels: 0 us -> 72 us
  local copies, waits for them, and re-layouts: 33.5 us -> 9.51 us
  between operations: 13.9 us -> 0.75 us
  matrix products: 10.8 us -> 0 us
  starting transfers between devices: 8.26 us -> 0 us
  other arithmetic: 7.9 us -> 0 us
    reduce_scatter x2 -> x0, waiting for transfers between devices: 101 us -> none  [the longest x1 63.1 us: local(): lax.psum_scatter(stacked.astype(jnp.bfloat16), 'dp', scatter_dimension=0,...]
    pallas_call x0 -> x1, Pallas kernels: none -> 72 us  [fused_local(): pl.pallas_call(fused, out_shape=(jax.ShapeDtypeStruct((tokens, features),...]
    all_to_all x2 -> x0, waiting for transfers between devices: 41.8 us -> none  [the longest x1 41.8 us: local(): lax.all_to_all(expert_rows, 'expert', split_axis=0, concat_axis=0, tiled=...]
    gather x10 -> x0, local copies, waits for them, and re-layouts: 22.1 us -> none  [the longest x2 15.5 us: combine(): jnp.take(returned.reshape(experts * capacity, features), flat_index, axis=0)]
    dot_general x3 -> x0, matrix products: 10.8 us -> none  [the longest x1 4.18 us: combine(): jnp.dot(d_logits, router_weight.astype(jnp.float32).T, precision=lax.Prec...]
    all_to_all x2 -> x0, starting transfers between devices: 8.14 us -> none  [the longest x1 4.81 us: local(): lax.all_to_all(expert_rows, 'expert', split_axis=0, concat_axis=0, tiled=...]
    select_n x2 -> x0, other arithmetic: 5.63 us -> none  [combine(): jnp.take(returned.reshape(experts * capacity, features), flat_index, axis=0)]
    reshape x2 -> x0, local copies, waits for them, and re-layouts: 3.77 us -> none  [the longest x1 3.68 us: combine(): returned.reshape(experts * capacity, features)]
  transfers between devices with their start and end apart: 5 -> 0, of which waited for: 3 -> 0; matrix products, arithmetic and copies ran while one was open for 18% -> 0% of each run, Pallas kernels for 0% -> 0%
where the time goes in v1:
time: 83.4 us; the launch traced here: 82.3 us
  Pallas kernels  72 us (86%)
  local copies, waits for them, and re-layouts  9.51 us (11%)
    pallas_call x1, Pallas kernels, fused_local(): pl.pallas_call(fused, out_shape=(jax.ShapeDtypeStruct((tokens, features),...  72 us
    unnamed x20, local copies, waits for them, and re-layouts  9.51 us

profile of v1, /device:TPU:0, one launch (start us, length us, event | category | flops | bytes accessed | tf_op | source)
XLA Modules:
  0.0 82.3 jit_solution(15991564676996064385)
XLA Ops:
  0.6 0.8 copy.14.routing_ref
  1.4 0.8 copy.15.base_ref
  2.2 1.2 %copy.16.router_ref = bf16[3072,8]{1,0:T(8,128)(2,1)S(1)} copy(bf16[3072,8]{0,1:T(8,128)(2,1)} %param.14) | data formatting | bytes 98304 | tf_op args[4]
  3.4 0.0 copy-start
  3.4 0.0 copy-start.1
  3.4 0.0 copy-start.2
  3.4 0.0 copy-start.3
  3.4 0.0 copy-start.4
  3.4 0.0 copy-start.5
  3.5 3.8 %copy.17.rows_hbm = bf16[8,66,3072]{2,1,0:T(8,128)(2,1)S(1)} copy(bf16[8,66,3072]{2,0,1:T(8,128)(2,1)} %param.15) | data formatting | bytes 6488064 | tf_op args[5]
  7.3 0.0 copy-done
  7.3 0.0 copy-done.1
  7.3 0.0 copy-done.2
  7.3 0.0 copy-done.3
  7.3 0.0 copy-done.4
  7.3 0.0 copy-done.5
  7.3 72.0 %shard_map.129 = (bf16[128,3072]{1,0:T(8,128)(2,1)S(1)}, f32[96,512]{1,0:T(8,128)S(1)}, f32[96,512]{1,0:T(8,128)S(1)}, f32[96,512]{1,0:T(8,128)S(1)}) custom-call(bf16[128,3072]{1,0:T(8,128)(2,1)S(1)} %copy-done, bf16[128,512]{1,0:T(8,128)(2,1)S(1)} %copy-done.4, s32[128,4]{1,0:T(8,128)S(1)} %copy.14.routing_ref, f32[128,8]{1,0:T(8,128)S(1)} %copy.15.base_ref, ...), custom_call_target="tpu_custom_call" | custom-call | flops 4000000000 | bytes 10000000 | tf_op jit(solution)/shard_map/pallas_call | solution.py:436
  79.4 0.9 %copy.22 = bf16[128,3072]{1,0:T(8,128)(2,1)} copy(bf16[128,3072]{1,0:T(8,128)(2,1)S(1)} %get-tuple-element.8) | data formatting | bytes 1572864
  80.3 0.7 copy.23
  80.9 0.7 copy.24
  81.6 0.7 copy.25
Async XLA Ops:
  3.4 3.9 %copy-start = (bf16[128,3072]{1,0:T(8,128)(2,1)S(1)}, bf16[128,3072]{1,0:T(8,128)(2,1)}, u32[]{:S(2)}) copy-start(bf16[128,3072]{1,0:T(8,128)(2,1)} %attn_hbm.1) | copy-start | bytes 2359300
  3.4 3.9 %copy-start.1 = (f32[96,512]{1,0:T(8,128)S(1)}, f32[96,512]{1,0:T(8,128)}, u32[]{:S(2)}) copy-start(f32[96,512]{1,0:T(8,128)} %weight_ref.1) | copy-start | bytes 589828
  3.4 3.9 %copy-start.2 = (f32[96,512]{1,0:T(8,128)S(1)}, f32[96,512]{1,0:T(8,128)}, u32[]{:S(2)}) copy-start(f32[96,512]{1,0:T(8,128)} %first_ref.1) | copy-start | bytes 589828
  3.4 3.9 %copy-start.3 = (f32[96,512]{1,0:T(8,128)S(1)}, f32[96,512]{1,0:T(8,128)}, u32[]{:S(2)}) copy-start(f32[96,512]{1,0:T(8,128)} %second_ref.1) | copy-start | bytes 589828
  3.4 3.9 %copy-start.4 = (bf16[128,512]{1,0:T(8,128)(2,1)S(1)}, bf16[128,512]{1,0:T(8,128)(2,1)}, u32[]{:S(2)}) copy-start(bf16[128,512]{1,0:T(8,128)(2,1)} %cot_ref.1) | copy-start | bytes 393220
  3.4 3.9 %copy-start.5 = (bf16[8,66]{1,0:T(8,128)(2,1)S(1)}, bf16[8,66]{1,0:T(8,128)(2,1)}, u32[]{:S(2)}) copy-start(bf16[8,66]{1,0:T(8,128)(2,1)} %dots_ref.1) | copy-start | bytes 3172

commit v2 on v0

--- a/solution.py
+++ b/solution.py
@@ -1,6 +1,8 @@
 import jax
 import jax.numpy as jnp
 from jax import lax
+from jax.experimental import pallas as pl
+from jax.experimental.pallas import tpu as pltpu
 from jax.sharding import PartitionSpec as P
 
 ADAM_STEP = 10
@@ -104,7 +106,470 @@
     return (input_grad, new_key_weight, new_first_moment, new_second_moment)
 
 
+MESH = pl.DeviceIdType.MESH
+CONTRACT_FIRST = (((0,), (0,)), ((), ()))
+CONTRACT_LAST = (((1,), (1,)), ((), ()))
+SLOTS = 80
+
+
+def split_columns(values):
+    high = values.astype(jnp.bfloat16)
+    low = (values - high.astype(jnp.float32)).astype(jnp.bfloat16)
+    return jnp.concatenate([high, low], axis=1)
+
+
+def fused(
+    attn_ref,
+    cot_ref,
+    routing_ref,
+    base_ref,
+    router_ref,
+    rows_hbm,
+    dots_ref,
+    weight_ref,
+    out_ref,
+    grad_ref,
+    rows_own,
+    picked,
+    blocks,
+    info_send,
+    info_got,
+    dots_send,
+    dots_got,
+    cots,
+    attn_send,
+    attn_got,
+    window,
+    part,
+    send,
+    relay_got,
+    x_got,
+    y_got,
+    grad_send,
+    grad_got,
+    local_sem,
+    info_ss,
+    info_rs,
+    rows_ss,
+    rows_rs,
+    dots_ss,
+    dots_rs,
+    cot_ss,
+    cot_rs,
+    twin_ss,
+    twin_rs,
+    attn_ss,
+    attn_rs,
+    wz_ss,
+    wz_rs,
+    wt_ss,
+    wt_rs,
+    part_ss,
+    part_rs,
+    gz_ss,
+    gz_rs,
+):
+    tokens, features = out_ref.shape
+    experts, capacity = dots_ref.shape
+    shard, keys = weight_ref.shape
+    layers = window.shape[0]
+    slab = features // layers
+    half = features // 2
+    z, e = lax.axis_index("dp"), lax.axis_index("expert")
+    y, x, c = e // 4, (e // 2) % 2, e % 2
+    chip = e // 2
+
+    def peer(r):
+        return ((y + r // 4) % 2) * 4 + ((x + (r // 2) % 2) % 2) * 2 + (c + r % 2) % 2
+
+    def columns(start, size):
+        return pl.ds(pl.multiple_of(start, 128), size)
+
+    def remote(src, dst, send_sem, recv_sem, to):
+        copy = pltpu.make_async_remote_copy(
+            src_ref=src,
+            dst_ref=dst,
+            send_sem=send_sem,
+            recv_sem=recv_sem,
+            device_id=to,
+            device_id_type=MESH,
+        )
+        copy.start()
+        return copy
+
+    barrier = pltpu.get_barrier_semaphore()
+    for r in range(1, experts):
+        pl.semaphore_signal(barrier, inc=1, device_id=(z, peer(r)), device_id_type=MESH)
+    for rz in range(1, layers):
+        pl.semaphore_signal(
+            barrier, inc=1, device_id=((z + rz) % layers, e), device_id_type=MESH
+        )
+    load = pltpu.make_async_copy(rows_hbm, rows_own, local_sem)
+    load.start()
+
+    shift = 64 * (chip % 2)
+
+    def window_rows(core):
+        return pl.ds(pl.multiple_of(shift + core * shard, 32), shard)
+
+    window[z, window_rows(c), :] = weight_ref[...].astype(jnp.bfloat16)
+    spare = pl.ds(pl.multiple_of(2 * shard * (1 - chip % 2), 64), 64)
+    for i in range(layers):
+        window[i, spare, :] = jnp.zeros((64, keys), jnp.bfloat16)
+
+    routing = routing_ref[...]
+    names = lax.broadcasted_iota(jnp.int32, (experts, tokens), 0)
+    choose = jnp.zeros((experts, tokens), jnp.float32)
+    for k in range(routing.shape[0]):
+        choose = choose + (routing[k : k + 1, :] == names).astype(jnp.float32)
+    earlier = (
+        lax.broadcasted_iota(jnp.int32, (tokens, tokens), 0)
+        < lax.broadcasted_iota(jnp.int32, (tokens, tokens), 1)
+    ).astype(jnp.bfloat16)
+    before = jnp.dot(choose.astype(jnp.bfloat16), earlier, preferred_element_type=jnp.float32)
+    place = jnp.where(choose > 0.0, before, -1.0)
+    logits = base_ref[...] + routed_offset * choose
+    raised = jnp.exp(logits - jnp.max(logits, axis=0, keepdims=True))
+    probs = raised / jnp.sum(raised, axis=0, keepdims=True)
+    chosen = probs * choose
+    chosen_sum = jnp.sum(chosen, axis=0, keepdims=True)
+    gate = chosen / chosen_sum
+    info_send[0] = place
+    info_send[1] = gate
+
+    dots_all = dots_ref[...].astype(jnp.float32)
+    dots_send[...] = jnp.zeros_like(dots_send)
+    for j in range(experts):
+        dots_send[j, :, 0:capacity] = jnp.broadcast_to(dots_all[j : j + 1, :], (8, capacity))
+    cots[0] = cot_ref[...]
+    for j in range(experts):
+        attn_send[j] = jnp.concatenate(
+            [
+                attn_ref[:, i * slab + j * shard : i * slab + (j + 1) * shard]
+                for i in range(layers)
+            ],
+            axis=1,
+        )
+    attn_got[0] = attn_send[e]
+    pl.semaphore_wait(barrier, experts - 1 + layers - 1)
+
+    twin = (z, peer(1))
+    info, cot, attn, dots, rows = {}, {}, {}, {}, {}
+    for q in (3, 1, 2):
+        info[q] = remote(
+            info_send, info_got.at[q], info_ss.at[q], info_rs.at[q], (z, peer(2 * q))
+        )
+    mine = window.at[z, window_rows(c)]
+    along = [
+        remote(mine, mine, wz_ss.at[rz], wz_rs.at[rz], ((z + rz) % layers, e))
+        for rz in range(1, layers)
+    ]
+    for q in (3, 1, 2):
+        cot[q] = remote(
+            cot_ref, cots.at[2 * q], cot_ss.at[q], cot_rs.at[q], (z, peer(2 * q))
+        )
+    for r in (6, 7, 2, 3, 4, 5, 1):
+        attn[r] = remote(
+            attn_send.at[peer(r)], attn_got.at[r], attn_ss.at[r], attn_rs.at[r], (z, peer(r))
+        )
+        dots[r] = remote(
+            dots_send.at[peer(r)], dots_got.at[r], dots_ss.at[r], dots_rs.at[r], (z, peer(r))
+        )
+
+    load.wait()
+    cell = lax.broadcasted_iota(jnp.int32, (SLOTS, experts * capacity), 1)
+    first_cell = experts * lax.broadcasted_iota(jnp.int32, (SLOTS, experts * capacity), 0)
+    pick = jnp.concatenate(
+        [
+            (cell == first_cell + peer(r)).astype(jnp.float32).astype(jnp.bfloat16)
+            for r in (1, 3, 5, 7, 0, 2, 4, 6)
+        ],
+        axis=0,
+    )
+
+    def pick_tile(i, _):
+        here = columns(i * slab, slab)
+        got = jnp.dot(pick, rows_own[:, here], preferred_element_type=jnp.float32)
+        for q in range(4):
+            picked[q, :, here] = got[q * SLOTS : (q + 1) * SLOTS].astype(jnp.bfloat16)
+            blocks[q, 0:SLOTS, here] = got[(4 + q) * SLOTS : (5 + q) * SLOTS].astype(
+                jnp.bfloat16
+            )
+        return 0
+
+    lax.fori_loop(0, layers, pick_tile, 0)
+    for q in (3, 1, 2, 0):
+        rows[q] = remote(
+            picked.at[q],
+            blocks.at[q, pl.ds(SLOTS, SLOTS)],
+            rows_ss.at[q],
+            rows_rs.at[q],
+            twin,
+        )
+
+    for copy in along:
+        copy.wait_recv()
+    column = window.at[:, window_rows(c)]
+    swap = remote(column, column, wt_ss, wt_rs, twin)
+    forward = {0: remote(cots.at[0], cots.at[1], twin_ss.at[0], twin_rs.at[0], twin)}
+
+    slots = lax.broadcasted_iota(jnp.int32, (SLOTS, tokens), 0)
+
+    def row_of(values, expert):
+        return jnp.sum(jnp.where(names == expert, values, 0.0), axis=0, keepdims=True)
+
+    def add_rows(q):
+        if q:
+            info[q].wait_recv()
+            place_q, gate_q = info_got[q, 0], info_got[q, 1]
+        else:
+            place_q, gate_q = place, gate
+        share = jnp.concatenate(
+            [
+                jnp.where(
+                    slots == row_of(place_q, expert).astype(jnp.int32),
+                    row_of(gate_q, expert),
+                    0.0,
+                )
+                for expert in (e, peer(1))
+            ],
+            axis=0,
+        )
+        share = split_columns(share)
+        rows[q].wait_recv()
+
+        def tile(i, _):
+            here = columns(i * slab, slab)
+            both = lax.dot_general(
+                share, blocks[q, :, here], CONTRACT_FIRST, preferred_element_type=jnp.float32
+            )
+            part[q, :, here] = both[:tokens] + both[tokens:]
+            return 0
+
+        lax.fori_loop(0, layers, tile, 0)
+
+    start = (chip * 2 * shard) // 128 * 128
+    width = window.shape[1]
+
+    def add_key(q):
+        def tile(i, _):
+            here = columns(i * slab + start, width)
+            part[q, :, here] += lax.dot_general(
+                cots[2 * q], window[i], CONTRACT_LAST, preferred_element_type=jnp.float32
+            )
+            return 0
+
+        lax.fori_loop(0, layers, tile, 0)
+
+    left, right = slice(0, half), slice(half, features)
+    to_x, to_y = (z, peer(2)), (z, peer(4))
+    parts = []
+
+    def send_part(q, cut, dst, number, to):
+        parts.append(
+            remote(
+                send.at[q, :, pl.ds(cut.start, half)],
+                dst.at[:, pl.ds(cut.start, half)],
+                part_ss.at[number],
+                part_rs.at[number],
+                to,
+            )
+        )
+
+    add_rows(3)
+    swap.wait_recv()
+    cot[3].wait_recv()
+    forward[3] = remote(cots.at[6], cots.at[7], twin_ss.at[3], twin_rs.at[3], twin)
+    add_key(3)
+    send[3] = part[3].astype(jnp.bfloat16)
+    send_part(3, left, relay_got, 0, to_x)
+    send_part(3, right, relay_got, 1, to_y)
+    for q, cut, dst, to in ((1, left, x_got, to_x), (2, right, y_got, to_y)):
+        add_rows(q)
+        cot[q].wait_recv()
+        forward[q] = remote(
+            cots.at[2 * q], cots.at[2 * q + 1], twin_ss.at[q], twin_rs.at[q], twin
+        )
+        add_key(q)
+        send[q, :, cut] = part[q, :, cut].astype(jnp.bfloat16)
+        send_part(q, cut, dst, q + 1, to)
+
+    for q in range(4):
+        forward[q].wait_recv()
+    for r in range(1, experts):
+        attn[r].wait_recv()
+    grad = lax.dot_general(
+        attn_got[...].reshape(experts * tokens, layers * shard),
+        cots[...].reshape(experts * tokens, keys),
+        CONTRACT_FIRST,
+        preferred_element_type=jnp.float32,
+    )
+    grad_send[...] = grad.reshape(layers, shard, keys).astype(jnp.bfloat16)
+    outward = {}
+    for rz in (2, 1, 3):
+        to = (z + rz) % layers
+        outward[rz] = remote(
+            grad_send.at[to], grad_got.at[rz], gz_ss.at[rz], gz_rs.at[rz], (to, e)
+        )
+    layer = lax.broadcasted_iota(jnp.int32, (layers, 1, 1), 0)
+    grad_ref[...] = jnp.sum(
+        jnp.where(layer == z, grad.reshape(layers, shard, keys), 0.0), axis=0
+    )
+
+    inner = jnp.zeros((experts, tokens), jnp.float32)
+    for r in range(experts):
+        if r > 0:
+            dots[r].wait_recv()
+            got = dots_got[r, :, 0:SLOTS]
+        else:
+            got = dots_send[e, :, 0:SLOTS]
+        expert = peer(r)
+        hit = (slots == row_of(place, expert).astype(jnp.int32)).astype(jnp.float32)
+        found = jnp.dot(
+            got.astype(jnp.bfloat16),
+            hit.astype(jnp.bfloat16),
+            preferred_element_type=jnp.float32,
+        )
+        inner = inner + jnp.where(names == expert, found[0:1, :], 0.0)
+    mean_inner = jnp.sum(gate * inner, axis=0, keepdims=True)
+    d_probs = choose * (inner - mean_inner) / chosen_sum
+    d_logits = probs * (d_probs - jnp.sum(probs * d_probs, axis=0, keepdims=True))
+    d_parts = split_columns(d_logits)
+
+    add_rows(0)
+    add_key(0)
+
+    def router_tile(i, _):
+        here = columns(i * slab, slab)
+        both = lax.dot_general(
+            d_parts, router_ref[:, here], CONTRACT_FIRST, preferred_element_type=jnp.float32
+        )
+        part[0, :, here] += both[:tokens] + both[tokens:]
+        return 0
+
+    lax.fori_loop(0, layers, router_tile, 0)
+
+    parts[0].wait_recv()
+    send[2, :, left] = (
+        part[2, :, left] + relay_got[:, left].astype(jnp.float32)
+    ).astype(jnp.bfloat16)
+    send_part(2, left, y_got, 4, to_y)
+    parts[1].wait_recv()
+    send[1, :, right] = (
+        part[1, :, right] + relay_got[:, right].astype(jnp.float32)
+    ).astype(jnp.bfloat16)
+    send_part(1, right, x_got, 5, to_x)
+
+    for rz in range(1, layers):
+        outward[rz].wait_recv()
+    grad_ref[...] = (
+        grad_ref[...]
+        + grad_got[1].astype(jnp.float32)
+        + grad_got[2].astype(jnp.float32)
+        + grad_got[3].astype(jnp.float32)
+    )
+    for copy in parts[2:]:
+        copy.wait_recv()
+    out_ref[...] = (
+        part[0] + x_got[...].astype(jnp.float32) + y_got[...].astype(jnp.float32)
+    ).astype(jnp.bfloat16)
+
+    for group in (info, cot, attn, dots, rows, forward, outward):
+        for copy in group.values():
+            copy.wait_send()
+    for copy in [*along, swap, *parts]:
+        copy.wait_send()
+
+
+def fused_local(
+    attn_input,
+    key_cot,
+    routing,
+    router_base,
+    router_weight,
+    expert_rows,
+    expert_dots,
+    key_weight,
+    first_moment,
+    second_moment,
+):
+    tokens, features = attn_input.shape
+    experts, capacity, _ = expert_rows.shape
+    shard, keys = key_weight.shape
+    layers = lax.axis_size("dp")
+    b16, f32 = jnp.bfloat16, jnp.float32
+    vmem, anywhere = pl.BlockSpec(memory_space=pltpu.VMEM), pl.BlockSpec(memory_space=pl.ANY)
+    dma = pltpu.SemaphoreType.DMA
+    input_grad, key_grad = pl.pallas_call(
+        fused,
+        out_shape=(
+            jax.ShapeDtypeStruct((tokens, features), b16),
+            jax.ShapeDtypeStruct((shard, keys), f32),
+        ),
+        in_specs=[vmem, vmem, vmem, vmem, vmem, anywhere, vmem, vmem],
+        out_specs=[vmem] * 2,
+        scratch_shapes=[
+            pltpu.VMEM((experts * capacity, features), b16),
+            pltpu.VMEM((4, SLOTS, features), b16),
+            pltpu.VMEM((4, 2 * SLOTS, features), b16),
+            pltpu.VMEM((2, experts, tokens), f32),
+            pltpu.VMEM((4, 2, experts, tokens), f32),
+            pltpu.VMEM((experts, 8, 128), f32),
+            pltpu.VMEM((experts, 8, 128), f32),
+            pltpu.VMEM((experts, tokens, keys), b16),
+            pltpu.VMEM((experts, tokens, layers * shard), b16),
+            pltpu.VMEM((experts, tokens, layers * shard), b16),
+            pltpu.VMEM((layers, 2 * shard + 64, keys), b16),
+            pltpu.VMEM((4, tokens, features), f32),
+            pltpu.VMEM((4, tokens, features), b16),
+            pltpu.VMEM((tokens, features), b16),
+            pltpu.VMEM((tokens, features), b16),
+            pltpu.VMEM((tokens, features), b16),
+            pltpu.VMEM((layers, shard, keys), b16),
+            pltpu.VMEM((layers, shard, keys), b16),
+            dma,
+            dma((4,)),
+            dma((4,)),
+            dma((4,)),
+            dma((4,)),
+            dma((experts,)),
+            dma((experts,)),
+            dma((4,)),
+            dma((4,)),
+            dma((4,)),
+            dma((4,)),
+            dma((experts,)),
+            dma((experts,)),
+            dma((layers,)),
+            dma((layers,)),
+            dma,
+            dma,
+            dma((6,)),
+            dma((6,)),
+            dma((layers,)),
+            dma((layers,)),
+        ],
+        compiler_params=pltpu.CompilerParams(
+            collective_id=0, has_side_effects=True, vmem_limit_bytes=48 * 1024 * 1024
+        ),
+        cost_estimate=pl.CostEstimate(
+            flops=6 * 10**9, bytes_accessed=10**7, transcendentals=10**4
+        ),
+    )(
+        attn_input,
+        key_cot,
+        routing.T,
+        router_base.T,
+        router_weight.T,
+        expert_rows.transpose(1, 0, 2).reshape(capacity * experts, features),
+        expert_dots,
+        key_weight,
+    )
+    return (input_grad, *adamw(key_weight, first_moment, second_moment, key_grad))
+
+
 def solution(mesh):
+    fits = mesh.shape["dp"] == 4 and mesh.shape["expert"] == 8
     in_specs = (
         P(("dp", "expert"), None),
         P(("dp", "expert"), None),
@@ -123,4 +588,5 @@
         P(("dp", "expert"), None),
         P(("dp", "expert"), None),
     )
-    return jax.shard_map(local, mesh=mesh, in_specs=in_specs, out_specs=out_specs, check_vma=False)
+    return jax.shard_map(
+        fused_local if fits else local, mesh=mesh, in_specs=in_specs, out_specs=out_specs, check_vma=False)

time: 218 us -> 58.7 us (0.27)
  waiting for transfers between devices: 143 us -> 0 us
  Pallas kernels: 0 us -> 48.2 us
  local copies, waits for them, and re-layouts: 33.5 us -> 8.61 us
  between operations: 13.9 us -> 0.68 us
  matrix products: 10.8 us -> 0 us
  starting transfers between devices: 8.26 us -> 0 us
  other arithmetic: 7.9 us -> 0.9 us
    reduce_scatter x2 -> x0, waiting for transfers between devices: 101 us -> none  [the longest x1 63.1 us: local(): lax.psum_scatter(stacked.astype(jnp.bfloat16), 'dp', scatter_dimension=0,...]
    pallas_call x0 -> x1, Pallas kernels: none -> 48.2 us  [fused_local(): pl.pallas_call(fused, out_shape=(jax.ShapeDtypeStruct((tokens, features),...]
    all_to_all x2 -> x0, waiting for transfers between devices: 41.8 us -> none  [the longest x1 41.8 us: local(): lax.all_to_all(expert_rows, 'expert', split_axis=0, concat_axis=0, tiled=...]
    gather x10 -> x0, local copies, waits for them, and re-layouts: 22.1 us -> none  [the longest x2 15.5 us: combine(): jnp.take(returned.reshape(experts * capacity, features), flat_index, axis=0)]
    dot_general x3 -> x0, matrix products: 10.8 us -> none  [the longest x1 4.18 us: combine(): jnp.dot(d_logits, router_weight.astype(jnp.float32).T, precision=lax.Prec...]
    all_to_all x2 -> x0, starting transfers between devices: 8.14 us -> none  [the longest x1 4.81 us: local(): lax.all_to_all(expert_rows, 'expert', split_axis=0, concat_axis=0, tiled=...]
    select_n x2 -> x0, other arithmetic: 5.63 us -> none  [combine(): jnp.take(returned.reshape(experts * capacity, features), flat_index, axis=0)]
    reshape x2 -> x0, local copies, waits for them, and re-layouts: 3.77 us -> none  [the longest x1 3.68 us: combine(): returned.reshape(experts * capacity, features)]
  transfers between devices with their start and end apart: 5 -> 0, of which waited for: 3 -> 0; matrix products, arithmetic and copies ran while one was open for 18% -> 0% of each run, Pallas kernels for 0% -> 0%
where the time goes in v2:
time: 58.7 us; the launch traced here: 58.3 us
  Pallas kernels  48.2 us (82%)
  local copies, waits for them, and re-layouts  8.61 us (15%)
  other arithmetic  0.9 us (2%)
  between operations  0.68 us (1%)
    pallas_call x1, Pallas kernels, fused_local(): pl.pallas_call(fused, out_shape=(jax.ShapeDtypeStruct((tokens, features),...  48.2 us
    unnamed x21, local copies, waits for them, and re-layouts  8.61 us

profile of v2, /device:TPU:0, one launch (start us, length us, event | category | flops | bytes accessed | tf_op | source)
XLA Modules:
  0.0 58.3 jit_solution(16039538587654502522)
XLA Ops:
  0.6 0.0 copy-start
  0.6 0.9 %copy-done = f32[96,512]{1,0:T(8,128)S(1)} copy-done((f32[96,512]{1,0:T(8,128)S(1)}, f32[96,512]{1,0:T(8,128)}, u32[]{:S(2)}) %copy-start) | copy-done | bytes 196632
  1.6 0.0 copy-start.1
  1.6 1.9 %copy-done.1 = bf16[8,66,3072]{2,0,1:T(8,128)(2,1)S(1)} copy-done((bf16[8,66,3072]{2,0,1:T(8,128)(2,1)S(1)}, bf16[8,66,3072]{2,0,1:T(8,128)(2,1)}, u32[]{:S(2)}) %copy-start.1) | copy-done | bytes 3244056
  3.5 0.0 copy-start.2
  3.5 1.1 %copy-done.2 = bf16[128,3072]{1,0:T(8,128)(2,1)S(1)} copy-done((bf16[128,3072]{1,0:T(8,128)(2,1)S(1)}, bf16[128,3072]{1,0:T(8,128)(2,1)}, u32[]{:S(2)}) %copy-start.2) | copy-done | bytes 786456
  4.6 0.0 copy-start.3
  4.6 0.9 %copy-done.3 = bf16[128,512]{1,0:T(8,128)(2,1)S(1)} copy-done((bf16[128,512]{1,0:T(8,128)(2,1)S(1)}, bf16[128,512]{1,0:T(8,128)(2,1)}, u32[]{:S(2)}) %copy-start.3) | copy-done | bytes 131096
  5.5 0.0 copy-start.4
  5.5 0.8 %copy-done.4 = bf16[3072,8]{0,1:T(8,128)(2,1)S(1)} copy-done((bf16[3072,8]{0,1:T(8,128)(2,1)S(1)}, bf16[3072,8]{0,1:T(8,128)(2,1)}, u32[]{:S(2)}) %copy-start.4) | copy-done | bytes 49176
  6.3 0.0 copy-start.5
  6.3 0.7 %copy-done.5 = f32[128,8]{0,1:T(8,128)S(1)} copy-done((f32[128,8]{0,1:T(8,128)S(1)}, f32[128,8]{0,1:T(8,128)}, u32[]{:S(2)}) %copy-start.5) | copy-done | bytes 4120
  7.0 0.0 copy-start.6
  7.0 0.7 %copy-done.6 = s32[128,4]{0,1:T(4,128)S(1)} copy-done((s32[128,4]{0,1:T(4,128)S(1)}, s32[128,4]{0,1:T(4,128)}, u32[]{:S(2)}) %copy-start.6) | copy-done | bytes 2072
  7.7 0.0 copy-start.7
  7.7 0.7 %copy-done.7 = bf16[8,66]{1,0:T(8,128)(2,1)S(1)} copy-done((bf16[8,66]{1,0:T(8,128)(2,1)S(1)}, bf16[8,66]{1,0:T(8,128)(2,1)}, u32[]{:S(2)}) %copy-start.7) | copy-done | bytes 1080
  8.4 0.0 copy-start.8
  8.4 0.0 copy-start.9
  8.4 48.2 %shard_map.129 = (bf16[128,3072]{1,0:T(8,128)(2,1)S(1)}, f32[96,512]{1,0:T(8,128)S(1)}) custom-call(bf16[128,3072]{1,0:T(8,128)(2,1)S(1)} %copy-done.2, bf16[128,512]{1,0:T(8,128)(2,1)S(1)} %copy-done.3, s32[4,128]{1,0:T(4,128)S(1)} %bitcast.9, f32[8,128]{1,0:T(8,128)S(1)} %bitcast.8, bf16[8,3072]{1,0:T(8,128)(2,1)S(1)} %bitcast.7, ...), custom_call_target="tpu_custom_call" | custom-call | flops 6000000000 | bytes 10000000 | tf_op jit(solution)/shard_map/pallas_call | solution.py:503
  56.5 0.0 copy-done.8
  56.6 0.0 copy-done.9
  56.6 0.9 %multiply_subtract_fusion = (f32[96,512]{1,0:T(8,128)}, f32[96,512]{1,0:T(8,128)}, f32[96,512]{1,0:T(8,128)}) fusion(f32[96,512]{1,0:T(8,128)S(1)} %copy-done, f32[96,512]{1,0:T(8,128)S(1)} %get-tuple-element.7, f32[96,512]{1,0:T(8,128)S(1)} %copy-done.8, f32[96,512]{1,0:T(8,128)S(1)} %copy-done.9), kind=kLoop, calls=%fused_computation.2 | loop fusion | flops 737280 | bytes 1376256 | tf_op jit(solution)/shard_map/sub | solution.py:61
  57.5 0.9 %copy.15 = bf16[128,3072]{1,0:T(8,128)(2,1)} copy(bf16[128,3072]{1,0:T(8,128)(2,1)S(1)} %get-tuple-element.15) | data formatting | bytes 1572864
Async XLA Ops:
  0.6 0.9 %copy-start = (f32[96,512]{1,0:T(8,128)S(1)}, f32[96,512]{1,0:T(8,128)}, u32[]{:S(2)}) copy-start(f32[96,512]{1,0:T(8,128)} %weight_ref.1) | copy-start | bytes 589828
  1.6 1.9 %copy-start.1 = (bf16[8,66,3072]{2,0,1:T(8,128)(2,1)S(1)}, bf16[8,66,3072]{2,0,1:T(8,128)(2,1)}, u32[]{:S(2)}) copy-start(bf16[8,66,3072]{2,0,1:T(8,128)(2,1)} %param.15) | copy-start | bytes 9732100
  3.5 1.1 %copy-start.2 = (bf16[128,3072]{1,0:T(8,128)(2,1)S(1)}, bf16[128,3072]{1,0:T(8,128)(2,1)}, u32[]{:S(2)}) copy-start(bf16[128,3072]{1,0:T(8,128)(2,1)} %attn_ref.1) | copy-start | bytes 2359300
  4.6 0.9 %copy-start.3 = (bf16[128,512]{1,0:T(8,128)(2,1)S(1)}, bf16[128,512]{1,0:T(8,128)(2,1)}, u32[]{:S(2)}) copy-start(bf16[128,512]{1,0:T(8,128)(2,1)} %cot_ref.1) | copy-start | bytes 393220
  5.5 0.8 %copy-start.4 = (bf16[3072,8]{0,1:T(8,128)(2,1)S(1)}, bf16[3072,8]{0,1:T(8,128)(2,1)}, u32[]{:S(2)}) copy-start(bf16[3072,8]{0,1:T(8,128)(2,1)} %param.14) | copy-start | bytes 147460
  6.3 0.7 %copy-start.5 = (f32[128,8]{0,1:T(8,128)S(1)}, f32[128,8]{0,1:T(8,128)}, u32[]{:S(2)}) copy-start(f32[128,8]{0,1:T(8,128)} %param.13) | copy-start | bytes 12292
  7.0 0.7 %copy-start.6 = (s32[128,4]{0,1:T(4,128)S(1)}, s32[128,4]{0,1:T(4,128)}, u32[]{:S(2)}) copy-start(s32[128,4]{0,1:T(4,128)} %param.12) | copy-start | bytes 6148
  7.7 0.7 %copy-start.7 = (bf16[8,66]{1,0:T(8,128)(2,1)S(1)}, bf16[8,66]{1,0:T(8,128)(2,1)}, u32[]{:S(2)}) copy-start(bf16[8,66]{1,0:T(8,128)(2,1)} %dots_ref.1) | copy-start | bytes 3172
  8.4 48.2 %copy-start.8 = (f32[96,512]{1,0:T(8,128)S(1)}, f32[96,512]{1,0:T(8,128)}, u32[]{:S(2)}) copy-start(f32[96,512]{1,0:T(8,128)} %param.18) | copy-start | bytes 589828
  8.4 48.2 %copy-start.9 = (f32[96,512]{1,0:T(8,128)S(1)}, f32[96,512]{1,0:T(8,128)}, u32[]{:S(2)}) copy-start(f32[96,512]{1,0:T(8,128)} %param.19) | copy-start | bytes 589828

commit v3 on v2

--- a/solution.py
+++ b/solution.py
@@ -119,16 +119,22 @@
 
 
 def fused(
+    attn_hbm,
+    cot_hbm,
+    routing_hbm,
+    base_hbm,
+    router_hbm,
+    rows_hbm,
+    dots_hbm,
+    weight_hbm,
+    out_ref,
+    grad_ref,
     attn_ref,
-    cot_ref,
     routing_ref,
     base_ref,
     router_ref,
-    rows_hbm,
     dots_ref,
     weight_ref,
-    out_ref,
-    grad_ref,
     rows_own,
     picked,
     blocks,
@@ -204,14 +210,31 @@
         pl.semaphore_signal(
             barrier, inc=1, device_id=((z + rz) % layers, e), device_id_type=MESH
         )
-    load = pltpu.make_async_copy(rows_hbm, rows_own, local_sem)
-    load.start()
+    loads = [
+        pltpu.make_async_copy(src, dst, local_sem.at[i])
+        for i, (src, dst) in enumerate(
+            (
+                (routing_hbm, routing_ref),
+                (base_hbm, base_ref),
+                (weight_hbm, weight_ref),
+                (dots_hbm, dots_ref),
+                (cot_hbm, cots.at[0]),
+                (attn_hbm, attn_ref),
+                (rows_hbm, rows_own),
+                (router_hbm, router_ref),
+            )
+        )
+    ]
+    for load in loads:
+        load.start()
 
     shift = 64 * (chip % 2)
 
     def window_rows(core):
         return pl.ds(pl.multiple_of(shift + core * shard, 32), shard)
 
+    for load in loads[:4]:
+        load.wait()
     window[z, window_rows(c), :] = weight_ref[...].astype(jnp.bfloat16)
     spare = pl.ds(pl.multiple_of(2 * shard * (1 - chip % 2), 64), 64)
     for i in range(layers):
@@ -241,7 +264,7 @@
     dots_send[...] = jnp.zeros_like(dots_send)
     for j in range(experts):
         dots_send[j, :, 0:capacity] = jnp.broadcast_to(dots_all[j : j + 1, :], (8, capacity))
-    cots[0] = cot_ref[...]
+    loads[5].wait()
     for j in range(experts):
         attn_send[j] = jnp.concatenate(
             [
@@ -251,6 +274,7 @@
             axis=1,
         )
     attn_got[0] = attn_send[e]
+    loads[4].wait()
     pl.semaphore_wait(barrier, experts - 1 + layers - 1)
 
     twin = (z, peer(1))
@@ -266,7 +290,7 @@
     ]
     for q in (3, 1, 2):
         cot[q] = remote(
-            cot_ref, cots.at[2 * q], cot_ss.at[q], cot_rs.at[q], (z, peer(2 * q))
+            cots.at[0], cots.at[2 * q], cot_ss.at[q], cot_rs.at[q], (z, peer(2 * q))
         )
     for r in (6, 7, 2, 3, 4, 5, 1):
         attn[r] = remote(
@@ -276,36 +300,41 @@
             dots_send.at[peer(r)], dots_got.at[r], dots_ss.at[r], dots_rs.at[r], (z, peer(r))
         )
 
-    load.wait()
+    loads[6].wait()
     cell = lax.broadcasted_iota(jnp.int32, (SLOTS, experts * capacity), 1)
     first_cell = experts * lax.broadcasted_iota(jnp.int32, (SLOTS, experts * capacity), 0)
-    pick = jnp.concatenate(
-        [
-            (cell == first_cell + peer(r)).astype(jnp.float32).astype(jnp.bfloat16)
-            for r in (1, 3, 5, 7, 0, 2, 4, 6)
-        ],
-        axis=0,
-    )
-
-    def pick_tile(i, _):
-        here = columns(i * slab, slab)
-        got = jnp.dot(pick, rows_own[:, here], preferred_element_type=jnp.float32)
-        for q in range(4):
-            picked[q, :, here] = got[q * SLOTS : (q + 1) * SLOTS].astype(jnp.bfloat16)
-            blocks[q, 0:SLOTS, here] = got[(4 + q) * SLOTS : (5 + q) * SLOTS].astype(
-                jnp.bfloat16
+
+    def pick_rows(group):
+        pick = jnp.concatenate(
+            [
+                (cell == first_cell + peer(r)).astype(jnp.float32).astype(jnp.bfloat16)
+                for q in group
+                for r in (2 * q + 1, 2 * q)
+            ],
+            axis=0,
+        )
+
+        def tile(i, _):
+            here = columns(i * slab, slab)
+            got = jnp.dot(pick, rows_own[:, here], preferred_element_type=jnp.float32)
+            got = got.astype(jnp.bfloat16)
+            for k, q in enumerate(group):
+                picked[q, :, here] = got[2 * k * SLOTS : (2 * k + 1) * SLOTS]
+                blocks[q, 0:SLOTS, here] = got[(2 * k + 1) * SLOTS : (2 * k + 2) * SLOTS]
+            return 0
+
+        lax.fori_loop(0, layers, tile, 0)
+        for q in group:
+            rows[q] = remote(
+                picked.at[q],
+                blocks.at[q, pl.ds(SLOTS, SLOTS)],
+                rows_ss.at[q],
+                rows_rs.at[q],
+                twin,
             )
-        return 0
-
-    lax.fori_loop(0, layers, pick_tile, 0)
-    for q in (3, 1, 2, 0):
-        rows[q] = remote(
-            picked.at[q],
-            blocks.at[q, pl.ds(SLOTS, SLOTS)],
-            rows_ss.at[q],
-            rows_rs.at[q],
-            twin,
-        )
+
+    pick_rows((3,))
+    pick_rows((1, 2, 0))
 
     for copy in along:
         copy.wait_recv()
@@ -438,6 +467,8 @@
 
     add_rows(0)
     add_key(0)
+
+    loads[7].wait()
 
     def router_tile(i, _):
         here = columns(i * slab, slab)
@@ -506,9 +537,15 @@
             jax.ShapeDtypeStruct((tokens, features), b16),
             jax.ShapeDtypeStruct((shard, keys), f32),
         ),
-        in_specs=[vmem, vmem, vmem, vmem, vmem, anywhere, vmem, vmem],
+        in_specs=[anywhere] * 8,
         out_specs=[vmem] * 2,
         scratch_shapes=[
+            pltpu.VMEM((tokens, features), b16),
+            pltpu.VMEM(routing.shape[::-1], jnp.int32),
+            pltpu.VMEM(router_base.shape[::-1], f32),
+            pltpu.VMEM(router_weight.shape[::-1], b16),
+            pltpu.VMEM(expert_dots.shape, b16),
+            pltpu.VMEM((shard, keys), f32),
             pltpu.VMEM((experts * capacity, features), b16),
             pltpu.VMEM((4, SLOTS, features), b16),
             pltpu.VMEM((4, 2 * SLOTS, features), b16),
@@ -527,7 +564,7 @@
             pltpu.VMEM((tokens, features), b16),
             pltpu.VMEM((layers, shard, keys), b16),
             pltpu.VMEM((layers, shard, keys), b16),
-            dma,
+            dma((8,)),
             dma((4,)),
             dma((4,)),
             dma((4,)),
@@ -550,7 +587,7 @@
             dma((layers,)),
         ],
         compiler_params=pltpu.CompilerParams(
-            collective_id=0, has_side_effects=True, vmem_limit_bytes=48 * 1024 * 1024
+            collective_id=0, has_side_effects=True, vmem_limit_bytes=60 * 1024 * 1024
         ),
         cost_estimate=pl.CostEstimate(
             flops=6 * 10**9, bytes_accessed=10**7, transcendentals=10**4

time: 58.7 us -> 54 us (0.920)
  local copies, waits for them, and re-layouts: 8.61 us -> 2.07 us
  Pallas kernels: 48.2 us -> 49.3 us
  other arithmetic: 0.9 us -> 1.82 us
    unnamed x21 -> x7, local copies, waits for them, and re-layouts: 8.61 us -> 2.07 us
    pallas_call x1, Pallas kernels: 48.2 us -> 49.3 us  [fused_local(): pl.pallas_call(fused, out_shape=(jax.ShapeDtypeStruct((tokens, features),...]
    sub x1, other arithmetic: 0.9 us -> 1.82 us  [adamw(): weight - learn_rate * (first_hat / (jnp.sqrt(second_hat) + epsilon) + dec...]
where the time goes in v3:
time: 54 us; the launch traced here: 53.9 us
  Pallas kernels  49.3 us (91%)
  local copies, waits for them, and re-layouts  2.07 us (4%)
  other arithmetic  1.82 us (3%)
  between operations  0.69 us (1%)
    pallas_call x1, Pallas kernels, fused_local(): pl.pallas_call(fused, out_shape=(jax.ShapeDtypeStruct((tokens, features),...  49.3 us
    unnamed x7, local copies, waits for them, and re-layouts  2.07 us
    sub x1, other arithmetic, adamw(): weight - learn_rate * (first_hat / (jnp.sqrt(second_hat) + epsilon) + dec...  1.82 us

profile of v3, /device:TPU:0, one launch (start us, length us, event | category | flops | bytes accessed | tf_op | source)
XLA Modules:
  0.0 53.9 jit_solution(14060781777186306103)
XLA Ops:
  0.6 0.0 copy-start
  0.6 0.0 copy-start.1
  0.7 0.0 copy-start.2
  0.7 49.3 %shard_map.129 = (bf16[128,3072]{1,0:T(8,128)(2,1)}, f32[96,512]{1,0:T(8,128)}) custom-call(bf16[128,3072]{1,0:T(8,128)(2,1)} %attn_hbm.1, bf16[128,512]{1,0:T(8,128)(2,1)} %cot_hbm.1, s32[4,128]{1,0:T(4,128)} %bitcast.9, f32[8,128]{1,0:T(8,128)} %bitcast.8, bf16[8,3072]{1,0:T(8,128)(2,1)} %bitcast.7, bf16[528,3072]{1,0:T(8,128)(2,1)} %bitcast.6, ...), custom_call_target="tpu_custom_call" | custom-call | flops 6000000000 | bytes 10000000 | tf_op jit(solution)/shard_map/pallas_call | solution.py:534
  49.9 0.0 copy-done
  50.0 0.0 copy-done.1
  50.0 0.0 copy-done.2
  50.0 1.8 %multiply_subtract_fusion = (f32[96,512]{1,0:T(8,128)}, f32[96,512]{1,0:T(8,128)}, f32[96,512]{1,0:T(8,128)}) fusion(f32[96,512]{1,0:T(8,128)S(1)} %copy-done, f32[96,512]{1,0:T(8,128)} %get-tuple-element.7, f32[96,512]{1,0:T(8,128)S(1)} %copy-done.1, f32[96,512]{1,0:T(8,128)S(1)} %copy-done.2), kind=kLoop, calls=%fused_computation.2 | loop fusion | flops 737280 | bytes 1376256 | tf_op jit(solution)/shard_map/sub | solution.py:61
  51.8 2.1 %copy.15 = bf16[128,3072]{1,0:T(8,128)(2,1)} copy(bf16[128,3072]{1,0:T(8,128)(2,1)} %get-tuple-element.15) | data formatting | bytes 1572864
Async XLA Ops:
  0.6 49.3 %copy-start = (f32[96,512]{1,0:T(8,128)S(1)}, f32[96,512]{1,0:T(8,128)}, u32[]{:S(2)}) copy-start(f32[96,512]{1,0:T(8,128)} %weight_hbm.1) | copy-start | bytes 589828
  0.6 49.3 %copy-start.1 = (f32[96,512]{1,0:T(8,128)S(1)}, f32[96,512]{1,0:T(8,128)}, u32[]{:S(2)}) copy-start(f32[96,512]{1,0:T(8,128)} %param.18) | copy-start | bytes 589828
  0.7 49.3 %copy-start.2 = (f32[96,512]{1,0:T(8,128)S(1)}, f32[96,512]{1,0:T(8,128)}, u32[]{:S(2)}) copy-start(f32[96,512]{1,0:T(8,128)} %param.19) | copy-start | bytes 589828

commit v4 on v3

--- a/solution.py
+++ b/solution.py
@@ -151,8 +151,11 @@
     relay_got,
     x_got,
     y_got,
+    grad_own,
     grad_send,
     grad_got,
+    cross_send,
+    cross_got,
     local_sem,
     info_ss,
     info_rs,
@@ -174,6 +177,8 @@
     part_rs,
     gz_ss,
     gz_rs,
+    gx_ss,
+    gx_rs,
 ):
     tokens, features = out_ref.shape
     experts, capacity = dots_ref.shape
@@ -265,15 +270,22 @@
     for j in range(experts):
         dots_send[j, :, 0:capacity] = jnp.broadcast_to(dots_all[j : j + 1, :], (8, capacity))
     loads[5].wait()
-    for j in range(experts):
-        attn_send[j] = jnp.concatenate(
-            [
-                attn_ref[:, i * slab + j * shard : i * slab + (j + 1) * shard]
-                for i in range(layers)
-            ],
-            axis=1,
-        )
-    attn_got[0] = attn_send[e]
+    bit = shard // 2
+    for across in range(2):
+        for near in range(2):
+            for core in range(2):
+                starts = [
+                    i * slab
+                    + (near * (4, 2)[1 - across] + far * (4, 2)[across] + core) * shard
+                    + across * bit
+                    for i in range(layers)
+                    for far in range(2)
+                ]
+                attn_send[across, near * 2 + core] = jnp.concatenate(
+                    [attn_ref[:, start : start + bit] for start in starts], axis=1
+                )
+    attn_got[0, 0] = attn_send[0, x * 2 + c]
+    attn_got[1, 0] = attn_send[1, y * 2 + c]
     loads[4].wait()
     pl.semaphore_wait(barrier, experts - 1 + layers - 1)
 
@@ -292,10 +304,17 @@
         cot[q] = remote(
             cots.at[0], cots.at[2 * q], cot_ss.at[q], cot_rs.at[q], (z, peer(2 * q))
         )
-    for r in (6, 7, 2, 3, 4, 5, 1):
-        attn[r] = remote(
-            attn_send.at[peer(r)], attn_got.at[r], attn_ss.at[r], attn_rs.at[r], (z, peer(r))
-        )
+    for across, place_to, r in ((0, 2, 2), (1, 2, 4), (0, 3, 3), (1, 3, 5), (0, 1, 1), (1, 1, 1)):
+        to, number = peer(r), across * 4 + place_to
+        near = (to // 2) % 2 if across == 0 else to // 4
+        attn[number] = remote(
+            attn_send.at[across, near * 2 + to % 2],
+            attn_got.at[across, place_to],
+            attn_ss.at[number],
+            attn_rs.at[number],
+            (z, to),
+        )
+    for r in range(1, experts):
         dots[r] = remote(
             dots_send.at[peer(r)], dots_got.at[r], dots_ss.at[r], dots_rs.at[r], (z, peer(r))
         )
@@ -408,42 +427,38 @@
     add_rows(3)
     swap.wait_recv()
     cot[3].wait_recv()
-    forward[3] = remote(cots.at[6], cots.at[7], twin_ss.at[3], twin_rs.at[3], twin)
     add_key(3)
     send[3] = part[3].astype(jnp.bfloat16)
     send_part(3, left, relay_got, 0, to_x)
     send_part(3, right, relay_got, 1, to_y)
-    for q, cut, dst, to in ((1, left, x_got, to_x), (2, right, y_got, to_y)):
-        add_rows(q)
+    for q in (1, 2):
         cot[q].wait_recv()
         forward[q] = remote(
             cots.at[2 * q], cots.at[2 * q + 1], twin_ss.at[q], twin_rs.at[q], twin
         )
-        add_key(q)
-        send[q, :, cut] = part[q, :, cut].astype(jnp.bfloat16)
-        send_part(q, cut, dst, q + 1, to)
-
-    for q in range(4):
-        forward[q].wait_recv()
-    for r in range(1, experts):
-        attn[r].wait_recv()
-    grad = lax.dot_general(
-        attn_got[...].reshape(experts * tokens, layers * shard),
-        cots[...].reshape(experts * tokens, keys),
-        CONTRACT_FIRST,
-        preferred_element_type=jnp.float32,
-    )
-    grad_send[...] = grad.reshape(layers, shard, keys).astype(jnp.bfloat16)
+    for copy in [*forward.values(), *attn.values()]:
+        copy.wait_recv()
+    for across in range(2):
+        near_cots = jnp.concatenate([cots[0:2], cots[2 + 2 * across : 4 + 2 * across]], axis=0)
+        grad = lax.dot_general(
+            attn_got[across].reshape(4 * tokens, layers * shard),
+            near_cots.reshape(4 * tokens, keys),
+            CONTRACT_FIRST,
+            preferred_element_type=jnp.float32,
+        ).reshape(layers, shard, keys)
+        grad_own[:, across * shard : (across + 1) * shard, :] = grad
+        grad_send[:, across * shard : (across + 1) * shard, :] = grad.astype(jnp.bfloat16)
     outward = {}
     for rz in (2, 1, 3):
         to = (z + rz) % layers
         outward[rz] = remote(
             grad_send.at[to], grad_got.at[rz], gz_ss.at[rz], gz_rs.at[rz], (to, e)
         )
-    layer = lax.broadcasted_iota(jnp.int32, (layers, 1, 1), 0)
-    grad_ref[...] = jnp.sum(
-        jnp.where(layer == z, grad.reshape(layers, shard, keys), 0.0), axis=0
-    )
+    for q, cut, dst, to in ((1, left, x_got, to_x), (2, right, y_got, to_y)):
+        add_rows(q)
+        add_key(q)
+        send[q, :, cut] = part[q, :, cut].astype(jnp.bfloat16)
+        send_part(q, cut, dst, q + 1, to)
 
     inner = jnp.zeros((experts, tokens), jnp.float32)
     for r in range(experts):
@@ -493,19 +508,36 @@
 
     for rz in range(1, layers):
         outward[rz].wait_recv()
-    grad_ref[...] = (
-        grad_ref[...]
+    grad_own[0] = (
+        grad_own[z]
         + grad_got[1].astype(jnp.float32)
         + grad_got[2].astype(jnp.float32)
         + grad_got[3].astype(jnp.float32)
     )
+    final = {}
+    for across, mine_o, r in ((0, y, 4), (1, x, 2)):
+        other = pl.ds(pl.multiple_of(across * shard + (1 - mine_o) * bit, 16), bit)
+        cross_send[across] = grad_own[0, other, :].astype(jnp.bfloat16)
+        final[across] = remote(
+            cross_send.at[across],
+            cross_got.at[across],
+            gx_ss.at[across],
+            gx_rs.at[across],
+            (z, peer(r)),
+        )
+    for across, mine_o in ((0, y), (1, x)):
+        final[across].wait_recv()
+        kept = pl.ds(pl.multiple_of(across * shard + mine_o * bit, 16), bit)
+        grad_ref[across * bit : (across + 1) * bit, :] = grad_own[0, kept, :] + cross_got[
+            across
+        ].astype(jnp.float32)
     for copy in parts[2:]:
         copy.wait_recv()
     out_ref[...] = (
         part[0] + x_got[...].astype(jnp.float32) + y_got[...].astype(jnp.float32)
     ).astype(jnp.bfloat16)
 
-    for group in (info, cot, attn, dots, rows, forward, outward):
+    for group in (info, cot, attn, dots, rows, forward, outward, final):
         for copy in group.values():
             copy.wait_send()
     for copy in [*along, swap, *parts]:
@@ -534,8 +566,8 @@
     input_grad, key_grad = pl.pallas_call(
         fused,
         out_shape=(
-            jax.ShapeDtypeStruct((tokens, features), b16),
-            jax.ShapeDtypeStruct((shard, keys), f32),
+            pltpu.VMEM((tokens, features), b16),
+            pltpu.VMEM((shard, keys), f32),
         ),
         in_specs=[anywhere] * 8,
         out_specs=[vmem] * 2,
@@ -554,16 +586,19 @@
             pltpu.VMEM((experts, 8, 128), f32),
             pltpu.VMEM((experts, 8, 128), f32),
             pltpu.VMEM((experts, tokens, keys), b16),
-            pltpu.VMEM((experts, tokens, layers * shard), b16),
-            pltpu.VMEM((experts, tokens, layers * shard), b16),
+            pltpu.VMEM((2, 4, tokens, layers * shard), b16),
+            pltpu.VMEM((2, 4, tokens, layers * shard), b16),
             pltpu.VMEM((layers, 2 * shard + 64, keys), b16),
             pltpu.VMEM((4, tokens, features), f32),
             pltpu.VMEM((4, tokens, features), b16),
             pltpu.VMEM((tokens, features), b16),
             pltpu.VMEM((tokens, features), b16),
             pltpu.VMEM((tokens, features), b16),
-            pltpu.VMEM((layers, shard, keys), b16),
-            pltpu.VMEM((layers, shard, keys), b16),
+            pltpu.VMEM((layers, 2 * shard, keys), f32),
+            pltpu.VMEM((layers, 2 * shard, keys), b16),
+            pltpu.VMEM((layers, 2 * shard, keys), b16),
+            pltpu.VMEM((2, shard // 2, keys), b16),
+            pltpu.VMEM((2, shard // 2, keys), b16),
             dma((8,)),
             dma((4,)),
             dma((4,)),
@@ -585,6 +620,8 @@
             dma((6,)),
             dma((layers,)),
             dma((layers,)),
+            dma((2,)),
+            dma((2,)),
         ],
         compiler_params=pltpu.CompilerParams(
             collective_id=0, has_side_effects=True, vmem_limit_bytes=60 * 1024 * 1024

time: 54 us -> 49.5 us (0.917)
  Pallas kernels: 49.3 us -> 46.9 us
  local copies, waits for them, and re-layouts: 2.07 us -> 0.89 us
  other arithmetic: 1.82 us -> 0.9 us
    pallas_call x1, Pallas kernels: 49.3 us -> 46.9 us  [fused_local(): pl.pallas_call(fused, out_shape=(pltpu.VMEM((tokens, features), b16), plt...]
    unnamed x7, local copies, waits for them, and re-layouts: 2.07 us -> 0.89 us
    sub x1, other arithmetic: 1.82 us -> 0.9 us  [adamw(): weight - learn_rate * (first_hat / (jnp.sqrt(second_hat) + epsilon) + dec...]
where the time goes in v4:
time: 49.5 us; the launch traced here: 49.3 us
  Pallas kernels  46.9 us (95%)
  other arithmetic  0.9 us (2%)
  local copies, waits for them, and re-layouts  0.89 us (2%)
  between operations  0.67 us (1%)
    pallas_call x1, Pallas kernels, fused_local(): pl.pallas_call(fused, out_shape=(pltpu.VMEM((tokens, features), b16), plt...  46.9 us

profile of v4, /device:TPU:0, one launch (start us, length us, event | category | flops | bytes accessed | tf_op | source)
XLA Modules:
  0.0 49.3 jit_solution(7891789086370386035)
XLA Ops:
  0.6 0.0 copy-start
  0.6 0.0 copy-start.1
  0.7 0.0 copy-start.2
  0.7 46.9 %shard_map.129 = (bf16[128,3072]{1,0:T(8,128)(2,1)S(1)}, f32[96,512]{1,0:T(8,128)S(1)}) custom-call(bf16[128,3072]{1,0:T(8,128)(2,1)} %attn_hbm.1, bf16[128,512]{1,0:T(8,128)(2,1)} %cot_hbm.1, s32[4,128]{1,0:T(4,128)} %bitcast.9, f32[8,128]{1,0:T(8,128)} %bitcast.8, bf16[8,3072]{1,0:T(8,128)(2,1)} %bitcast.7, bf16[528,3072]{1,0:T(8,128)(2,1)} %bitcast.6, ...), custom_call_target="tpu_custom_call" | custom-call | flops 6000000000 | bytes 10000000 | tf_op jit(solution)/shard_map/pallas_call | solution.py:566
  47.5 0.9 %copy.15 = bf16[128,3072]{1,0:T(8,128)(2,1)} copy(bf16[128,3072]{1,0:T(8,128)(2,1)S(1)} %get-tuple-element.11) | data formatting | bytes 1572864
  48.4 0.0 copy-done
  48.4 0.0 copy-done.1
  48.4 0.0 copy-done.2
  48.4 0.9 %multiply_subtract_fusion = (f32[96,512]{1,0:T(8,128)}, f32[96,512]{1,0:T(8,128)}, f32[96,512]{1,0:T(8,128)}) fusion(f32[96,512]{1,0:T(8,128)S(1)} %copy-done, f32[96,512]{1,0:T(8,128)S(1)} %get-tuple-element.7, f32[96,512]{1,0:T(8,128)S(1)} %copy-done.1, f32[96,512]{1,0:T(8,128)S(1)} %copy-done.2), kind=kLoop, calls=%fused_computation.2 | loop fusion | flops 737280 | bytes 1376256 | tf_op jit(solution)/shard_map/sub | solution.py:61
Async XLA Ops:
  0.6 47.8 %copy-start = (f32[96,512]{1,0:T(8,128)S(1)}, f32[96,512]{1,0:T(8,128)}, u32[]{:S(2)}) copy-start(f32[96,512]{1,0:T(8,128)} %weight_hbm.1) | copy-start | bytes 589828
  0.6 47.8 %copy-start.1 = (f32[96,512]{1,0:T(8,128)S(1)}, f32[96,512]{1,0:T(8,128)}, u32[]{:S(2)}) copy-start(f32[96,512]{1,0:T(8,128)} %param.18) | copy-start | bytes 589828
  0.7 47.8 %copy-start.2 = (f32[96,512]{1,0:T(8,128)S(1)}, f32[96,512]{1,0:T(8,128)}, u32[]{:S(2)}) copy-start(f32[96,512]{1,0:T(8,128)} %param.19) | copy-start | bytes 589828

commit v5 on v4

--- a/solution.py
+++ b/solution.py
@@ -185,7 +185,6 @@
     shard, keys = weight_ref.shape
     layers = window.shape[0]
     slab = features // layers
-    half = features // 2
     z, e = lax.axis_index("dp"), lax.axis_index("expert")
     y, x, c = e // 4, (e // 2) % 2, e % 2
     chip = e // 2
@@ -269,6 +268,60 @@
     dots_send[...] = jnp.zeros_like(dots_send)
     for j in range(experts):
         dots_send[j, :, 0:capacity] = jnp.broadcast_to(dots_all[j : j + 1, :], (8, capacity))
+    loads[4].wait()
+    pl.semaphore_wait(barrier, experts - 1 + layers - 1)
+
+    twin = (z, peer(1))
+    info, cot, attn, dots, rows = {}, {}, {}, {}, {}
+    for q in (3, 1, 2):
+        info[q] = remote(
+            info_send, info_got.at[q], info_ss.at[q], info_rs.at[q], (z, peer(2 * q))
+        )
+    mine = window.at[z, window_rows(c)]
+    swap = {0: remote(mine, mine, wt_ss.at[0], wt_rs.at[0], twin)}
+    along = {
+        rz: remote(mine, mine, wz_ss.at[rz], wz_rs.at[rz], ((z + rz) % layers, e))
+        for rz in (3, 2, 1)
+    }
+    for q in (3, 1, 2):
+        cot[q] = remote(
+            cots.at[0], cots.at[2 * q], cot_ss.at[q], cot_rs.at[q], (z, peer(2 * q))
+        )
+    forward = {0: remote(cots.at[0], cots.at[1], twin_ss.at[0], twin_rs.at[0], twin)}
+    loads[6].wait()
+    cell = lax.broadcasted_iota(jnp.int32, (SLOTS, experts * capacity), 1)
+    first_cell = experts * lax.broadcasted_iota(jnp.int32, (SLOTS, experts * capacity), 0)
+
+    def pick_rows(group):
+        pick = jnp.concatenate(
+            [
+                (cell == first_cell + peer(r)).astype(jnp.float32).astype(jnp.bfloat16)
+                for q in group
+                for r in (2 * q + 1, 2 * q)
+            ],
+            axis=0,
+        )
+
+        def tile(i, _):
+            here = columns(i * slab, slab)
+            got = jnp.dot(pick, rows_own[:, here], preferred_element_type=jnp.float32)
+            got = got.astype(jnp.bfloat16)
+            for k, q in enumerate(group):
+                picked[q, :, here] = got[2 * k * SLOTS : (2 * k + 1) * SLOTS]
+                blocks[q, 0:SLOTS, here] = got[(2 * k + 1) * SLOTS : (2 * k + 2) * SLOTS]
+            return 0
+
+        lax.fori_loop(0, layers, tile, 0)
+        for q in group:
+            rows[q] = remote(
+                picked.at[q],
+                blocks.at[q, pl.ds(SLOTS, SLOTS)],
+                rows_ss.at[q],
+                rows_rs.at[q],
+                twin,
+            )
+
+    pick_rows((3,))
     loads[5].wait()
     bit = shard // 2
     for across in range(2):
@@ -286,24 +339,6 @@
                 )
     attn_got[0, 0] = attn_send[0, x * 2 + c]
     attn_got[1, 0] = attn_send[1, y * 2 + c]
-    loads[4].wait()
-    pl.semaphore_wait(barrier, experts - 1 + layers - 1)
-
-    twin = (z, peer(1))
-    info, cot, attn, dots, rows = {}, {}, {}, {}, {}
-    for q in (3, 1, 2):
-        info[q] = remote(
-            info_send, info_got.at[q], info_ss.at[q], info_rs.at[q], (z, peer(2 * q))
-        )
-    mine = window.at[z, window_rows(c)]
-    along = [
-        remote(mine, mine, wz_ss.at[rz], wz_rs.at[rz], ((z + rz) % layers, e))
-        for rz in range(1, layers)
-    ]
-    for q in (3, 1, 2):
-        cot[q] = remote(
-            cots.at[0], cots.at[2 * q], cot_ss.at[q], cot_rs.at[q], (z, peer(2 * q))
-        )
     for across, place_to, r in ((0, 2, 2), (1, 2, 4), (0, 3, 3), (1, 3, 5), (0, 1, 1), (1, 1, 1)):
         to, number = peer(r), across * 4 + place_to
         near = (to // 2) % 2 if across == 0 else to // 4
@@ -319,54 +354,22 @@
             dots_send.at[peer(r)], dots_got.at[r], dots_ss.at[r], dots_rs.at[r], (z, peer(r))
         )
 
-    loads[6].wait()
-    cell = lax.broadcasted_iota(jnp.int32, (SLOTS, experts * capacity), 1)
-    first_cell = experts * lax.broadcasted_iota(jnp.int32, (SLOTS, experts * capacity), 0)
-
-    def pick_rows(group):
-        pick = jnp.concatenate(
-            [
-                (cell == first_cell + peer(r)).astype(jnp.float32).astype(jnp.bfloat16)
-                for q in group
-                for r in (2 * q + 1, 2 * q)
-            ],
-            axis=0,
-        )
-
-        def tile(i, _):
-            here = columns(i * slab, slab)
-            got = jnp.dot(pick, rows_own[:, here], preferred_element_type=jnp.float32)
-            got = got.astype(jnp.bfloat16)
-            for k, q in enumerate(group):
-                picked[q, :, here] = got[2 * k * SLOTS : (2 * k + 1) * SLOTS]
-                blocks[q, 0:SLOTS, here] = got[(2 * k + 1) * SLOTS : (2 * k + 2) * SLOTS]
-            return 0
-
-        lax.fori_loop(0, layers, tile, 0)
-        for q in group:
-            rows[q] = remote(
-                picked.at[q],
-                blocks.at[q, pl.ds(SLOTS, SLOTS)],
-                rows_ss.at[q],
-                rows_rs.at[q],
-                twin,
-            )
-
-    pick_rows((3,))
-    pick_rows((1, 2, 0))
-
-    for copy in along:
-        copy.wait_recv()
-    column = window.at[:, window_rows(c)]
-    swap = remote(column, column, wt_ss, wt_rs, twin)
-    forward = {0: remote(cots.at[0], cots.at[1], twin_ss.at[0], twin_rs.at[0], twin)}
-
+    pick_rows((1, 2))
+
+    def pass_on(k):
+        along[layers - k].wait_recv()
+        block = window.at[(z + k) % layers, window_rows(c)]
+        swap[k] = remote(block, block, wt_ss.at[k], wt_rs.at[k], twin)
+
+    pass_on(1)
     slots = lax.broadcasted_iota(jnp.int32, (SLOTS, tokens), 0)
 
     def row_of(values, expert):
         return jnp.sum(jnp.where(names == expert, values, 0.0), axis=0, keepdims=True)
 
-    def add_rows(q):
+    shares = {}
+
+    def make_share(q):
         if q:
             info[q].wait_recv()
             place_q, gate_q = info_got[q, 0], info_got[q, 1]
@@ -383,54 +386,55 @@
             ],
             axis=0,
         )
-        share = split_columns(share)
+        shares[q] = split_columns(share)
         rows[q].wait_recv()
-
-        def tile(i, _):
-            here = columns(i * slab, slab)
-            both = lax.dot_general(
-                share, blocks[q, :, here], CONTRACT_FIRST, preferred_element_type=jnp.float32
-            )
-            part[q, :, here] = both[:tokens] + both[tokens:]
-            return 0
-
-        lax.fori_loop(0, layers, tile, 0)
 
     start = (chip * 2 * shard) // 128 * 128
     width = window.shape[1]
 
-    def add_key(q):
-        def tile(i, _):
-            here = columns(i * slab + start, width)
-            part[q, :, here] += lax.dot_general(
-                cots[2 * q], window[i], CONTRACT_LAST, preferred_element_type=jnp.float32
-            )
-            return 0
-
-        lax.fori_loop(0, layers, tile, 0)
-
-    left, right = slice(0, half), slice(half, features)
+    def slab_of(k):
+        return columns(((z + k) % layers) * slab, slab)
+
+    def add_rows(q, k):
+        here = slab_of(k)
+        both = lax.dot_general(
+            shares[q], blocks[q, :, here], CONTRACT_FIRST, preferred_element_type=jnp.float32
+        )
+        part[q, :, here] = both[:tokens] + both[tokens:]
+
+    def add_key(q, k):
+        here = columns(((z + k) % layers) * slab + start, width)
+        part[q, :, here] += lax.dot_general(
+            cots[2 * q],
+            window[(z + k) % layers],
+            CONTRACT_LAST,
+            preferred_element_type=jnp.float32,
+        )
+
     to_x, to_y = (z, peer(2)), (z, peer(4))
-    parts = []
-
-    def send_part(q, cut, dst, number, to):
-        parts.append(
-            remote(
-                send.at[q, :, pl.ds(cut.start, half)],
-                dst.at[:, pl.ds(cut.start, half)],
-                part_ss.at[number],
-                part_rs.at[number],
-                to,
-            )
-        )
-
-    add_rows(3)
-    swap.wait_recv()
+    x_first = [(to_x, x_got), (to_y, y_got)]
+    relays, direct, onward = {}, {}, {}
+
+    def send_slab(q, k, dst, number, to):
+        here = slab_of(k)
+        return remote(
+            send.at[q, :, here], dst.at[:, here], part_ss.at[number], part_rs.at[number], to
+        )
+
+    make_share(3)
+    for k in range(layers):
+        add_rows(3, k)
     cot[3].wait_recv()
-    add_key(3)
-    send[3] = part[3].astype(jnp.bfloat16)
-    send_part(3, left, relay_got, 0, to_x)
-    send_part(3, right, relay_got, 1, to_y)
+    for k in range(layers):
+        swap[k].wait_recv()
+        add_key(3, k)
+        here = slab_of(k)
+        send[3, :, here] = part[3, :, here].astype(jnp.bfloat16)
+        relays[k] = send_slab(3, k, relay_got, k, x_first[k % 2][0])
+        if k == 0:
+            pass_on(2)
+            pass_on(3)
+
     for q in (1, 2):
         cot[q].wait_recv()
         forward[q] = remote(
@@ -454,12 +458,27 @@
         outward[rz] = remote(
             grad_send.at[to], grad_got.at[rz], gz_ss.at[rz], gz_rs.at[rz], (to, e)
         )
-    for q, cut, dst, to in ((1, left, x_got, to_x), (2, right, y_got, to_y)):
-        add_rows(q)
-        add_key(q)
-        send[q, :, cut] = part[q, :, cut].astype(jnp.bfloat16)
-        send_part(q, cut, dst, q + 1, to)
-
+    make_share(1)
+    make_share(2)
+    for k in range(layers):
+        q, (to, dst) = k % 2 + 1, x_first[k % 2]
+        add_rows(q, k)
+        add_key(q, k)
+        here = slab_of(k)
+        send[q, :, here] = part[q, :, here].astype(jnp.bfloat16)
+        direct[k] = send_slab(q, k, dst, layers + k, to)
+    for k in range(layers):
+        q, (to, dst) = 2 - k % 2, x_first[1 - k % 2]
+        add_rows(q, k)
+        add_key(q, k)
+        relays[k].wait_recv()
+        here = slab_of(k)
+        send[q, :, here] = (
+            part[q, :, here] + relay_got[:, here].astype(jnp.float32)
+        ).astype(jnp.bfloat16)
+        onward[k] = send_slab(q, k, dst, 2 * layers + k, to)
+
+    pick_rows((0,))
     inner = jnp.zeros((experts, tokens), jnp.float32)
     for r in range(experts):
         if r > 0:
@@ -480,8 +499,10 @@
     d_logits = probs * (d_probs - jnp.sum(probs * d_probs, axis=0, keepdims=True))
     d_parts = split_columns(d_logits)
 
-    add_rows(0)
-    add_key(0)
+    make_share(0)
+    for k in range(layers):
+        add_rows(0, k)
+        add_key(0, k)
 
     loads[7].wait()
 
@@ -494,17 +515,6 @@
         return 0
 
     lax.fori_loop(0, layers, router_tile, 0)
-
-    parts[0].wait_recv()
-    send[2, :, left] = (
-        part[2, :, left] + relay_got[:, left].astype(jnp.float32)
-    ).astype(jnp.bfloat16)
-    send_part(2, left, y_got, 4, to_y)
-    parts[1].wait_recv()
-    send[1, :, right] = (
-        part[1, :, right] + relay_got[:, right].astype(jnp.float32)
-    ).astype(jnp.bfloat16)
-    send_part(1, right, x_got, 5, to_x)
 
     for rz in range(1, layers):
         outward[rz].wait_recv()
@@ -525,23 +535,27 @@
             gx_rs.at[across],
             (z, peer(r)),
         )
+    for k in range(layers):
+        direct[k].wait_recv()
+        onward[k].wait_recv()
+        here = slab_of(k)
+        out_ref[:, here] = (
+            part[0, :, here]
+            + x_got[:, here].astype(jnp.float32)
+            + y_got[:, here].astype(jnp.float32)
+        ).astype(jnp.bfloat16)
     for across, mine_o in ((0, y), (1, x)):
         final[across].wait_recv()
         kept = pl.ds(pl.multiple_of(across * shard + mine_o * bit, 16), bit)
         grad_ref[across * bit : (across + 1) * bit, :] = grad_own[0, kept, :] + cross_got[
             across
         ].astype(jnp.float32)
-    for copy in parts[2:]:
-        copy.wait_recv()
-    out_ref[...] = (
-        part[0] + x_got[...].astype(jnp.float32) + y_got[...].astype(jnp.float32)
-    ).astype(jnp.bfloat16)
-
     for group in (info, cot, attn, dots, rows, forward, outward, final):
         for copy in group.values():
             copy.wait_send()
-    for copy in [*along, swap, *parts]:
-        copy.wait_send()
+    for group in (along, swap, relays, direct, onward):
+        for copy in group.values():
+            copy.wait_send()
 
 
 def fused_local(
@@ -614,10 +628,10 @@
             dma((experts,)),
             dma((layers,)),
             dma((layers,)),
-            dma,
-            dma,
-            dma((6,)),
-            dma((6,)),
+            dma((layers,)),
+            dma((layers,)),
+            dma((3 * layers,)),
+            dma((3 * layers,)),
             dma((layers,)),
             dma((layers,)),
             dma((2,)),

time: 49.5 us -> 47.7 us (0.964)
  Pallas kernels: 46.9 us -> 45.1 us
    pallas_call x1, Pallas kernels: 46.9 us -> 45.1 us  [fused_local(): pl.pallas_call(fused, out_shape=(pltpu.VMEM((tokens, features), b16), plt...]
where the time goes in v5:
time: 47.7 us; the launch traced here: 47.6 us
  Pallas kernels  45.1 us (95%)
  other arithmetic  0.9 us (2%)
  local copies, waits for them, and re-layouts  0.89 us (2%)
  between operations  0.67 us (1%)
    pallas_call x1, Pallas kernels, fused_local(): pl.pallas_call(fused, out_shape=(pltpu.VMEM((tokens, features), b16), plt...  45.1 us

profile of v5, /device:TPU:0, one launch (start us, length us, event | category | flops | bytes accessed | tf_op | source)
XLA Modules:
  0.0 47.6 jit_solution(6654233826334223848)
XLA Ops:
  0.6 0.0 copy-start
  0.6 0.0 copy-start.1
  0.7 0.0 copy-start.2
  0.7 45.1 %shard_map.129 = (bf16[128,3072]{1,0:T(8,128)(2,1)S(1)}, f32[96,512]{1,0:T(8,128)S(1)}) custom-call(bf16[128,3072]{1,0:T(8,128)(2,1)} %attn_hbm.1, bf16[128,512]{1,0:T(8,128)(2,1)} %cot_hbm.1, s32[4,128]{1,0:T(4,128)} %bitcast.9, f32[8,128]{1,0:T(8,128)} %bitcast.8, bf16[8,3072]{1,0:T(8,128)(2,1)} %bitcast.7, bf16[528,3072]{1,0:T(8,128)(2,1)} %bitcast.6, ...), custom_call_target="tpu_custom_call" | custom-call | flops 6000000000 | bytes 10000000 | tf_op jit(solution)/shard_map/pallas_call | solution.py:580
  45.8 0.9 %copy.15 = bf16[128,3072]{1,0:T(8,128)(2,1)} copy(bf16[128,3072]{1,0:T(8,128)(2,1)S(1)} %get-tuple-element.11) | data formatting | bytes 1572864
  46.7 0.0 copy-done
  46.7 0.0 copy-done.1
  46.7 0.0 copy-done.2
  46.7 0.9 %multiply_subtract_fusion = (f32[96,512]{1,0:T(8,128)}, f32[96,512]{1,0:T(8,128)}, f32[96,512]{1,0:T(8,128)}) fusion(f32[96,512]{1,0:T(8,128)S(1)} %copy-done, f32[96,512]{1,0:T(8,128)S(1)} %get-tuple-element.7, f32[96,512]{1,0:T(8,128)S(1)} %copy-done.1, f32[96,512]{1,0:T(8,128)S(1)} %copy-done.2), kind=kLoop, calls=%fused_computation.2 | loop fusion | flops 737280 | bytes 1376256 | tf_op jit(solution)/shard_map/sub | solution.py:61
Async XLA Ops:
  0.6 46.1 %copy-start = (f32[96,512]{1,0:T(8,128)S(1)}, f32[96,512]{1,0:T(8,128)}, u32[]{:S(2)}) copy-start(f32[96,512]{1,0:T(8,128)} %weight_hbm.1) | copy-start | bytes 589828
  0.6 46.0 %copy-start.1 = (f32[96,512]{1,0:T(8,128)S(1)}, f32[96,512]{1,0:T(8,128)}, u32[]{:S(2)}) copy-start(f32[96,512]{1,0:T(8,128)} %param.18) | copy-start | bytes 589828
  0.7 46.0 %copy-start.2 = (f32[96,512]{1,0:T(8,128)S(1)}, f32[96,512]{1,0:T(8,128)}, u32[]{:S(2)}) copy-start(f32[96,512]{1,0:T(8,128)} %param.19) | copy-start | bytes 589828

commit v6 on v5

--- a/solution.py
+++ b/solution.py
@@ -237,13 +237,30 @@
     def window_rows(core):
         return pl.ds(pl.multiple_of(shift + core * shard, 32), shard)
 
-    for load in loads[:4]:
-        load.wait()
+    loads[2].wait()
     window[z, window_rows(c), :] = weight_ref[...].astype(jnp.bfloat16)
     spare = pl.ds(pl.multiple_of(2 * shard * (1 - chip % 2), 64), 64)
     for i in range(layers):
         window[i, spare, :] = jnp.zeros((64, keys), jnp.bfloat16)
 
+    loads[4].wait()
+    pl.semaphore_wait(barrier, experts - 1 + layers - 1)
+
+    twin = (z, peer(1))
+    info, cot, attn, dots, rows = {}, {}, {}, {}, {}
+    mine = window.at[z, window_rows(c)]
+    swap = {0: remote(mine, mine, wt_ss.at[0], wt_rs.at[0], twin)}
+    along = {
+        rz: remote(mine, mine, wz_ss.at[rz], wz_rs.at[rz], ((z + rz) % layers, e))
+        for rz in (3, 2, 1)
+    }
+    for q in (1, 2):
+        cot[q] = remote(
+            cots.at[0], cots.at[2 * q], cot_ss.at[q], cot_rs.at[q], (z, peer(2 * q))
+        )
+    forward = {0: remote(cots.at[0], cots.at[1], twin_ss.at[0], twin_rs.at[0], twin)}
+    for i in (0, 1, 3):
+        loads[i].wait()
     routing = routing_ref[...]
     names = lax.broadcasted_iota(jnp.int32, (experts, tokens), 0)
     choose = jnp.zeros((experts, tokens), jnp.float32)
@@ -268,26 +285,10 @@
     dots_send[...] = jnp.zeros_like(dots_send)
     for j in range(experts):
         dots_send[j, :, 0:capacity] = jnp.broadcast_to(dots_all[j : j + 1, :], (8, capacity))
-    loads[4].wait()
-    pl.semaphore_wait(barrier, experts - 1 + layers - 1)
-
-    twin = (z, peer(1))
-    info, cot, attn, dots, rows = {}, {}, {}, {}, {}
     for q in (3, 1, 2):
         info[q] = remote(
             info_send, info_got.at[q], info_ss.at[q], info_rs.at[q], (z, peer(2 * q))
         )
-    mine = window.at[z, window_rows(c)]
-    swap = {0: remote(mine, mine, wt_ss.at[0], wt_rs.at[0], twin)}
-    along = {
-        rz: remote(mine, mine, wz_ss.at[rz], wz_rs.at[rz], ((z + rz) % layers, e))
-        for rz in (3, 2, 1)
-    }
-    for q in (3, 1, 2):
-        cot[q] = remote(
-            cots.at[0], cots.at[2 * q], cot_ss.at[q], cot_rs.at[q], (z, peer(2 * q))
-        )
-    forward = {0: remote(cots.at[0], cots.at[1], twin_ss.at[0], twin_rs.at[0], twin)}
     loads[6].wait()
     cell = lax.broadcasted_iota(jnp.int32, (SLOTS, experts * capacity), 1)
     first_cell = experts * lax.broadcasted_iota(jnp.int32, (SLOTS, experts * capacity), 0)
@@ -322,6 +323,19 @@
             )
 
     pick_rows((3,))
+    for q in (1, 2):
+        cot[q].wait_recv()
+        piece = pl.ds((q - 1) * (tokens // 2), tokens // 2)
+        cot[2 + q] = remote(
+            cots.at[2 * q, piece],
+            cots.at[6, piece],
+            cot_ss.at[2 + q],
+            cot_rs.at[2 + q],
+            (z, peer(6 - 2 * q)),
+        )
+        forward[q] = remote(
+            cots.at[2 * q], cots.at[2 * q + 1], twin_ss.at[q], twin_rs.at[q], twin
+        )
     loads[5].wait()
     bit = shard // 2
     for across in range(2):
@@ -354,7 +368,6 @@
             dots_send.at[peer(r)], dots_got.at[r], dots_ss.at[r], dots_rs.at[r], (z, peer(r))
         )
 
-    pick_rows((1, 2))
 
     def pass_on(k):
         along[layers - k].wait_recv()
@@ -425,21 +438,18 @@
     for k in range(layers):
         add_rows(3, k)
     cot[3].wait_recv()
+    cot[4].wait_recv()
     for k in range(layers):
         swap[k].wait_recv()
         add_key(3, k)
         here = slab_of(k)
         send[3, :, here] = part[3, :, here].astype(jnp.bfloat16)
         relays[k] = send_slab(3, k, relay_got, k, x_first[k % 2][0])
-        if k == 0:
+        if k == 1:
+            pick_rows((1, 2))
             pass_on(2)
             pass_on(3)
 
-    for q in (1, 2):
-        cot[q].wait_recv()
-        forward[q] = remote(
-            cots.at[2 * q], cots.at[2 * q + 1], twin_ss.at[q], twin_rs.at[q], twin
-        )
     for copy in [*forward.values(), *attn.values()]:
         copy.wait_recv()
     for across in range(2):
@@ -620,8 +630,8 @@
             dma((4,)),
             dma((experts,)),
             dma((experts,)),
-            dma((4,)),
-            dma((4,)),
+            dma((5,)),
+            dma((5,)),
             dma((4,)),
             dma((4,)),
             dma((experts,)),

time: 47.7 us -> 46.8 us (0.981)
  Pallas kernels: 45.1 us -> 44.2 us
    pallas_call x1, Pallas kernels: 45.1 us -> 44.2 us  [fused_local(): pl.pallas_call(fused, out_shape=(pltpu.VMEM((tokens, features), b16), plt...]
where the time goes in v6:
time: 46.8 us; the launch traced here: 46.6 us
  Pallas kernels  44.2 us (94%)
  other arithmetic  0.9 us (2%)
  local copies, waits for them, and re-layouts  0.89 us (2%)
  between operations  0.67 us (1%)
    pallas_call x1, Pallas kernels, fused_local(): pl.pallas_call(fused, out_shape=(pltpu.VMEM((tokens, features), b16), plt...  44.2 us

profile of v6, /device:TPU:0, one launch (start us, length us, event | category | flops | bytes accessed | tf_op | source)
XLA Modules:
  0.0 46.6 jit_solution(11924675071906777418)
XLA Ops:
  0.6 0.0 copy-start
  0.6 0.0 copy-start.1
  0.7 0.0 copy-start.2
  0.7 44.2 %shard_map.129 = (bf16[128,3072]{1,0:T(8,128)(2,1)S(1)}, f32[96,512]{1,0:T(8,128)S(1)}) custom-call(bf16[128,3072]{1,0:T(8,128)(2,1)} %attn_hbm.1, bf16[128,512]{1,0:T(8,128)(2,1)} %cot_hbm.1, s32[4,128]{1,0:T(4,128)} %bitcast.9, f32[8,128]{1,0:T(8,128)} %bitcast.8, bf16[8,3072]{1,0:T(8,128)(2,1)} %bitcast.7, bf16[528,3072]{1,0:T(8,128)(2,1)} %bitcast.6, ...), custom_call_target="tpu_custom_call" | custom-call | flops 6000000000 | bytes 10000000 | tf_op jit(solution)/shard_map/pallas_call | solution.py:590
  44.8 0.9 %copy.15 = bf16[128,3072]{1,0:T(8,128)(2,1)} copy(bf16[128,3072]{1,0:T(8,128)(2,1)S(1)} %get-tuple-element.11) | data formatting | bytes 1572864
  45.7 0.0 copy-done
  45.7 0.0 copy-done.1
  45.7 0.0 copy-done.2
  45.7 0.9 %multiply_subtract_fusion = (f32[96,512]{1,0:T(8,128)}, f32[96,512]{1,0:T(8,128)}, f32[96,512]{1,0:T(8,128)}) fusion(f32[96,512]{1,0:T(8,128)S(1)} %copy-done, f32[96,512]{1,0:T(8,128)S(1)} %get-tuple-element.7, f32[96,512]{1,0:T(8,128)S(1)} %copy-done.1, f32[96,512]{1,0:T(8,128)S(1)} %copy-done.2), kind=kLoop, calls=%fused_computation.2 | loop fusion | flops 737280 | bytes 1376256 | tf_op jit(solution)/shard_map/sub | solution.py:61
Async XLA Ops:
  0.6 45.1 %copy-start = (f32[96,512]{1,0:T(8,128)S(1)}, f32[96,512]{1,0:T(8,128)}, u32[]{:S(2)}) copy-start(f32[96,512]{1,0:T(8,128)} %weight_hbm.1) | copy-start | bytes 589828
  0.6 45.1 %copy-start.1 = (f32[96,512]{1,0:T(8,128)S(1)}, f32[96,512]{1,0:T(8,128)}, u32[]{:S(2)}) copy-start(f32[96,512]{1,0:T(8,128)} %param.18) | copy-start | bytes 589828
  0.7 45.1 %copy-start.2 = (f32[96,512]{1,0:T(8,128)S(1)}, f32[96,512]{1,0:T(8,128)}, u32[]{:S(2)}) copy-start(f32[96,512]{1,0:T(8,128)} %param.19) | copy-start | bytes 589828

commit v7 on v6

--- a/solution.py
+++ b/solution.py
@@ -399,7 +399,7 @@
             ],
             axis=0,
         )
-        shares[q] = split_columns(share)
+        shares[q] = share.astype(jnp.bfloat16)
         rows[q].wait_recv()
 
     start = (chip * 2 * shard) // 128 * 128
@@ -410,10 +410,9 @@
 
     def add_rows(q, k):
         here = slab_of(k)
-        both = lax.dot_general(
+        part[q, :, here] = lax.dot_general(
             shares[q], blocks[q, :, here], CONTRACT_FIRST, preferred_element_type=jnp.float32
         )
-        part[q, :, here] = both[:tokens] + both[tokens:]
 
     def add_key(q, k):
         here = columns(((z + k) % layers) * slab + start, width)
@@ -446,7 +445,6 @@
         send[3, :, here] = part[3, :, here].astype(jnp.bfloat16)
         relays[k] = send_slab(3, k, relay_got, k, x_first[k % 2][0])
         if k == 1:
-            pick_rows((1, 2))
             pass_on(2)
             pass_on(3)
 
@@ -468,6 +466,7 @@
         outward[rz] = remote(
             grad_send.at[to], grad_got.at[rz], gz_ss.at[rz], gz_rs.at[rz], (to, e)
         )
+    pick_rows((1, 2))
     make_share(1)
     make_share(2)
     for k in range(layers):

time: 46.8 us -> 47.3 us (1.011)
  Pallas kernels: 44.2 us -> 44.7 us
    pallas_call x1, Pallas kernels: 44.2 us -> 44.7 us  [fused_local(): pl.pallas_call(fused, out_shape=(pltpu.VMEM((tokens, features), b16), plt...]
where the time goes in v7:
time: 47.3 us; the launch traced here: 47.2 us
  Pallas kernels  44.7 us (95%)
  other arithmetic  0.9 us (2%)
  local copies, waits for them, and re-layouts  0.89 us (2%)
  between operations  0.67 us (1%)
    pallas_call x1, Pallas kernels, fused_local(): pl.pallas_call(fused, out_shape=(pltpu.VMEM((tokens, features), b16), plt...  44.7 us

profile of v7, /device:TPU:0, one launch (start us, length us, event | category | flops | bytes accessed | tf_op | source)
XLA Modules:
  0.0 47.2 jit_solution(1034793061440033682)
XLA Ops:
  0.6 0.0 copy-start
  0.6 0.0 copy-start.1
  0.7 0.0 copy-start.2
  0.7 44.7 %shard_map.129 = (bf16[128,3072]{1,0:T(8,128)(2,1)S(1)}, f32[96,512]{1,0:T(8,128)S(1)}) custom-call(bf16[128,3072]{1,0:T(8,128)(2,1)} %attn_hbm.1, bf16[128,512]{1,0:T(8,128)(2,1)} %cot_hbm.1, s32[4,128]{1,0:T(4,128)} %bitcast.9, f32[8,128]{1,0:T(8,128)} %bitcast.8, bf16[8,3072]{1,0:T(8,128)(2,1)} %bitcast.7, bf16[528,3072]{1,0:T(8,128)(2,1)} %bitcast.6, ...), custom_call_target="tpu_custom_call" | custom-call | flops 6000000000 | bytes 10000000 | tf_op jit(solution)/shard_map/pallas_call | solution.py:589
  45.4 0.9 %copy.15 = bf16[128,3072]{1,0:T(8,128)(2,1)} copy(bf16[128,3072]{1,0:T(8,128)(2,1)S(1)} %get-tuple-element.11) | data formatting | bytes 1572864
  46.3 0.0 copy-done
  46.3 0.0 copy-done.1
  46.3 0.0 copy-done.2
  46.3 0.9 %multiply_subtract_fusion = (f32[96,512]{1,0:T(8,128)}, f32[96,512]{1,0:T(8,128)}, f32[96,512]{1,0:T(8,128)}) fusion(f32[96,512]{1,0:T(8,128)S(1)} %copy-done, f32[96,512]{1,0:T(8,128)S(1)} %get-tuple-element.7, f32[96,512]{1,0:T(8,128)S(1)} %copy-done.1, f32[96,512]{1,0:T(8,128)S(1)} %copy-done.2), kind=kLoop, calls=%fused_computation.2 | loop fusion | flops 737280 | bytes 1376256 | tf_op jit(solution)/shard_map/sub | solution.py:61
Async XLA Ops:
  0.6 45.6 %copy-start = (f32[96,512]{1,0:T(8,128)S(1)}, f32[96,512]{1,0:T(8,128)}, u32[]{:S(2)}) copy-start(f32[96,512]{1,0:T(8,128)} %weight_hbm.1) | copy-start | bytes 589828
  0.6 45.6 %copy-start.1 = (f32[96,512]{1,0:T(8,128)S(1)}, f32[96,512]{1,0:T(8,128)}, u32[]{:S(2)}) copy-start(f32[96,512]{1,0:T(8,128)} %param.18) | copy-start | bytes 589828
  0.7 45.6 %copy-start.2 = (f32[96,512]{1,0:T(8,128)S(1)}, f32[96,512]{1,0:T(8,128)}, u32[]{:S(2)}) copy-start(f32[96,512]{1,0:T(8,128)} %param.19) | copy-start | bytes 589828

commit v8 on v7

--- a/solution.py
+++ b/solution.py
@@ -322,20 +322,6 @@
                 twin,
             )
 
-    pick_rows((3,))
-    for q in (1, 2):
-        cot[q].wait_recv()
-        piece = pl.ds((q - 1) * (tokens // 2), tokens // 2)
-        cot[2 + q] = remote(
-            cots.at[2 * q, piece],
-            cots.at[6, piece],
-            cot_ss.at[2 + q],
-            cot_rs.at[2 + q],
-            (z, peer(6 - 2 * q)),
-        )
-        forward[q] = remote(
-            cots.at[2 * q], cots.at[2 * q + 1], twin_ss.at[q], twin_rs.at[q], twin
-        )
     loads[5].wait()
     bit = shard // 2
     for across in range(2):
@@ -367,7 +353,20 @@
         dots[r] = remote(
             dots_send.at[peer(r)], dots_got.at[r], dots_ss.at[r], dots_rs.at[r], (z, peer(r))
         )
-
+    for q in (1, 2):
+        cot[q].wait_recv()
+        piece = pl.ds((q - 1) * (tokens // 2), tokens // 2)
+        cot[2 + q] = remote(
+            cots.at[2 * q, piece],
+            cots.at[6, piece],
+            cot_ss.at[2 + q],
+            cot_rs.at[2 + q],
+            (z, peer(6 - 2 * q)),
+        )
+        forward[q] = remote(
+            cots.at[2 * q], cots.at[2 * q + 1], twin_ss.at[q], twin_rs.at[q], twin
+        )
+    pick_rows((3,))
 
     def pass_on(k):
         along[layers - k].wait_recv()
@@ -434,11 +433,12 @@
         )
 
     make_share(3)
-    for k in range(layers):
-        add_rows(3, k)
+    add_rows(3, 0)
     cot[3].wait_recv()
     cot[4].wait_recv()
     for k in range(layers):
+        if k:
+            add_rows(3, k)
         swap[k].wait_recv()
         add_key(3, k)
         here = slab_of(k)

time: 47.3 us -> 48.4 us (1.023)
  Pallas kernels: 44.7 us -> 45.8 us
    pallas_call x1, Pallas kernels: 44.7 us -> 45.8 us  [fused_local(): pl.pallas_call(fused, out_shape=(pltpu.VMEM((tokens, features), b16), plt...]
where the time goes in v8:
time: 48.4 us; the launch traced here: 48.3 us
  Pallas kernels  45.8 us (95%)
  other arithmetic  0.9 us (2%)
  local copies, waits for them, and re-layouts  0.89 us (2%)
  between operations  0.67 us (1%)
    pallas_call x1, Pallas kernels, fused_local(): pl.pallas_call(fused, out_shape=(pltpu.VMEM((tokens, features), b16), plt...  45.8 us

profile of v8, /device:TPU:0, one launch (start us, length us, event | category | flops | bytes accessed | tf_op | source)
XLA Modules:
  0.0 48.3 jit_solution(13298321469524106053)
XLA Ops:
  0.6 0.0 copy-start
  0.6 0.0 copy-start.1
  0.7 0.0 copy-start.2
  0.7 45.8 %shard_map.129 = (bf16[128,3072]{1,0:T(8,128)(2,1)S(1)}, f32[96,512]{1,0:T(8,128)S(1)}) custom-call(bf16[128,3072]{1,0:T(8,128)(2,1)} %attn_hbm.1, bf16[128,512]{1,0:T(8,128)(2,1)} %cot_hbm.1, s32[4,128]{1,0:T(4,128)} %bitcast.9, f32[8,128]{1,0:T(8,128)} %bitcast.8, bf16[8,3072]{1,0:T(8,128)(2,1)} %bitcast.7, bf16[528,3072]{1,0:T(8,128)(2,1)} %bitcast.6, ...), custom_call_target="tpu_custom_call" | custom-call | flops 6000000000 | bytes 10000000 | tf_op jit(solution)/shard_map/pallas_call | solution.py:589
  46.5 0.9 %copy.15 = bf16[128,3072]{1,0:T(8,128)(2,1)} copy(bf16[128,3072]{1,0:T(8,128)(2,1)S(1)} %get-tuple-element.11) | data formatting | bytes 1572864
  47.4 0.0 copy-done
  47.4 0.0 copy-done.1
  47.4 0.0 copy-done.2
  47.4 0.9 %multiply_subtract_fusion = (f32[96,512]{1,0:T(8,128)}, f32[96,512]{1,0:T(8,128)}, f32[96,512]{1,0:T(8,128)}) fusion(f32[96,512]{1,0:T(8,128)S(1)} %copy-done, f32[96,512]{1,0:T(8,128)S(1)} %get-tuple-element.7, f32[96,512]{1,0:T(8,128)S(1)} %copy-done.1, f32[96,512]{1,0:T(8,128)S(1)} %copy-done.2), kind=kLoop, calls=%fused_computation.2 | loop fusion | flops 737280 | bytes 1376256 | tf_op jit(solution)/shard_map/sub | solution.py:61
Async XLA Ops:
  0.6 46.8 %copy-start = (f32[96,512]{1,0:T(8,128)S(1)}, f32[96,512]{1,0:T(8,128)}, u32[]{:S(2)}) copy-start(f32[96,512]{1,0:T(8,128)} %weight_hbm.1) | copy-start | bytes 589828
  0.6 46.8 %copy-start.1 = (f32[96,512]{1,0:T(8,128)S(1)}, f32[96,512]{1,0:T(8,128)}, u32[]{:S(2)}) copy-start(f32[96,512]{1,0:T(8,128)} %param.18) | copy-start | bytes 589828
  0.7 46.8 %copy-start.2 = (f32[96,512]{1,0:T(8,128)S(1)}, f32[96,512]{1,0:T(8,128)}, u32[]{:S(2)}) copy-start(f32[96,512]{1,0:T(8,128)} %param.19) | copy-start | bytes 589828
